TPU v7x, 32 devices: a whole 2x2x4 slice. The times are simulated.
32 devices in a mesh: dp: 8 (over y, x, core), mp: 4 (over z).
Axes of the slice: x: 2, y: 2, z: 4, core: 2. Of those that a mesh axis runs over, the one named last changes fastest.
Arguments:
- fields: bfloat16 [8, 128, 20, 128, 128], P('dp', 'mp'), may hold values from -6 to 6
- cotangent: bfloat16 [8, 128, 20, 128, 128], P('dp', 'mp'), may hold values from -3 to 3
- spectral_weight: bfloat16 [32, 2, 20, 20, 512], P('dp', None, None, None, 'mp'), may hold values from -5 to 5
- conv_weight: bfloat16 [20, 20], replicated, may hold values from -1.25 to 1.25
- conv_bias: float32 [20], replicated, may hold values from -3 to 3
Outputs:
- spectral_grad: float32 [32, 2, 20, 20, 512], P('dp', None, None, None, 'mp')
All inputs are finite; a program needn't handle non-finite values.
Results may differ from a plain program's by a relative error of at most 0.0085.
Values may be sent and summed in bfloat16 or wider, within the bound.
A program may use at most 320 MiB of HBM per device.

v0:
```python
import math

import jax
import jax.numpy as jnp
from jax import lax
from jax.sharding import PartitionSpec as P

X = 128
Y = 128
Z = 128
C = 20
KX = 32
KY = 32
KZ = 16


inv_root_two = 0.7071067811865476
inv_root_two_pi = 0.3989422804014327
highest = lax.Precision.HIGHEST


def kept_modes(count, length):
    indices = jnp.arange(count, dtype=jnp.int32)
    return jnp.where(indices < count // 2, indices, length - count + indices)


def gelu_slope(values):
    return (
        0.5 * (1.0 + lax.erf(values * inv_root_two))
        + values * jnp.exp(-0.5 * values * values) * inv_root_two_pi
    )


def dft_tables(kept, length):
    cells = jnp.arange(length, dtype=jnp.int32)
    phases = 2.0 * math.pi / length * (kept[:, None] * cells[None, :] % length).astype(jnp.float32)
    return (jnp.cos(phases), jnp.sin(phases))


def split_parts(values):
    upper = values.astype(jnp.bfloat16)
    lower = (values - upper.astype(jnp.float32)).astype(jnp.bfloat16)
    return (upper, lower)


def two_pass(form, data_bf, table_pair):
    first = jnp.einsum(form, data_bf, table_pair[0], preferred_element_type=jnp.float32)
    return first + jnp.einsum(form, data_bf, table_pair[1], preferred_element_type=jnp.float32)


def three_pass(form, data_f32, table_pair):
    data_hi, data_lo = split_parts(data_f32)
    total = jnp.einsum(form, data_hi, table_pair[0], preferred_element_type=jnp.float32)
    total = total + jnp.einsum(form, data_hi, table_pair[1], preferred_element_type=jnp.float32)
    return total + jnp.einsum(form, data_lo, table_pair[0], preferred_element_type=jnp.float32)


def mix_modes(modes_in, weights):
    spec_re = modes_in[..., 0, :, :]
    spec_im = modes_in[..., 1, :, :]
    real_w = weights[..., 0, :, :, :]
    imag_w = weights[..., 1, :, :, :]
    out_re = jnp.einsum("...cm,...com->...om", spec_re, real_w, precision=highest) - jnp.einsum(
        "...cm,...com->...om", spec_im, imag_w, precision=highest
    )
    out_im = jnp.einsum("...cm,...com->...om", spec_re, imag_w, precision=highest) + jnp.einsum(
        "...cm,...com->...om", spec_im, real_w, precision=highest
    )
    return jnp.stack([out_re, out_im], axis=-3)


def grad_term(modes_in, back_modes):
    spec_re = modes_in[..., 0, :, :]
    spec_im = modes_in[..., 1, :, :]
    back_re = back_modes[..., 0, :, :]
    back_im = back_modes[..., 1, :, :]
    grad_re = jnp.einsum("...cm,...om->...com", spec_re, back_re, precision=highest) + jnp.einsum(
        "...cm,...om->...com", spec_im, back_im, precision=highest
    )
    grad_im = jnp.einsum("...cm,...om->...com", spec_re, back_im, precision=highest) - jnp.einsum(
        "...cm,...om->...com", spec_im, back_re, precision=highest
    )
    return jnp.stack([grad_re, grad_im], axis=-4)


def shards(fields, cotangent, spectral_weight, conv_weight, conv_bias):
    slab_len = fields.shape[1]
    ky_local = KY // lax.axis_size("mp")
    data_count = lax.axis_size("dp")
    kx_local = spectral_weight.shape[0]
    cos_x, sin_x = dft_tables(kept_modes(KX, X), X)
    cos_y, sin_y = dft_tables(kept_modes(KY, Y), Y)
    modes_z = jnp.arange(KZ, dtype=jnp.int32)
    cos_z, sin_z = dft_tables(modes_z, Z)
    weight_z = jnp.where(modes_z == 0, 1.0, 2.0).astype(jnp.float32) / (X * Y * Z)
    table_y = split_parts(jnp.concatenate([cos_y.T, -sin_y.T], axis=1))
    table_z = jnp.concatenate([cos_z.T, -sin_z.T], axis=1)
    inverse_re = jnp.concatenate([weight_z[:, None] * cos_z, -weight_z[:, None] * sin_z], axis=0)
    inverse_im = jnp.concatenate([weight_z[:, None] * sin_z, weight_z[:, None] * cos_z], axis=0)
    inverse_y = split_parts(jnp.concatenate([cos_y, -sin_y], axis=0))
    scale_modes = jnp.tile(weight_z, ky_local)

    def forward_modes(volume):
        along_y = two_pass("xcyz,yk->xckz", volume, table_y)
        along_yz = jnp.einsum("xckz,zm->xckm", along_y, table_z, precision=highest)
        a_cos = along_yz[:, :, :KY, :KZ]
        a_sin = along_yz[:, :, :KY, KZ:]
        b_cos = along_yz[:, :, KY:, :KZ]
        b_sin = along_yz[:, :, KY:, KZ:]
        packed = jnp.stack([a_cos - b_sin, b_cos + a_sin], axis=3)
        packed = jnp.transpose(packed, (0, 2, 1, 3, 4)).reshape(slab_len, KY, -1)
        moved = lax.all_to_all(packed, "mp", split_axis=1, concat_axis=0, tiled=True)
        flat_modes = moved.reshape(X, -1)
        with_cos = jnp.dot(cos_x, flat_modes, precision=highest).reshape(KX, ky_local, C, 2, KZ)
        with_sin = jnp.dot(sin_x, flat_modes, precision=highest).reshape(KX, ky_local, C, 2, KZ)
        real_part = with_cos[:, :, :, 0] + with_sin[:, :, :, 1]
        imag_part = with_cos[:, :, :, 1] - with_sin[:, :, :, 0]
        stacked = jnp.stack([real_part, imag_part], axis=1)
        return jnp.transpose(stacked, (0, 1, 3, 2, 4)).reshape(KX, 2, C, ky_local * KZ)

    def across_samples(modes_in):
        moved = lax.all_to_all(
            modes_in.reshape(1, KX, -1), "dp", split_axis=1, concat_axis=0, tiled=True
        )
        return moved.reshape(data_count, kx_local, 2, C, -1)

    volume = fields[0]
    spectra = forward_modes(volume)
    conv_term = jnp.einsum("xcyz,co->xoyz", volume, conv_weight, preferred_element_type=jnp.float32)
    sample_spectra = across_samples(spectra)
    local_mixed = mix_modes(sample_spectra, spectral_weight.astype(jnp.float32))
    returned = lax.all_to_all(
        local_mixed.reshape(data_count, kx_local, -1), "dp", split_axis=0, concat_axis=1, tiled=True
    )
    mixed_modes = returned.reshape(KX, 2, C, -1)
    flat_mixed = mixed_modes.reshape(KX, -1)
    back_cos = jnp.dot(cos_x.T, flat_mixed, precision=highest).reshape(X, 2, C, ky_local, KZ)
    back_sin = jnp.dot(sin_x.T, flat_mixed, precision=highest).reshape(X, 2, C, ky_local, KZ)
    real_part = back_cos[:, 0] - back_sin[:, 1]
    imag_part = back_sin[:, 0] + back_cos[:, 1]
    outgoing = jnp.transpose(jnp.stack([real_part, imag_part], axis=3), (0, 2, 1, 3, 4)).reshape(
        X, ky_local, -1
    )
    slabs = lax.all_to_all(outgoing, "mp", split_axis=0, concat_axis=1, tiled=True).reshape(
        slab_len, KY, C, 2 * KZ
    )
    along_re = jnp.einsum("xkcm,mz->xkcz", slabs, inverse_re, precision=highest)
    along_im = jnp.einsum("xkcm,mz->xkcz", slabs, inverse_im, precision=highest)
    spectral = three_pass("xkcz,ky->xcyz", jnp.concatenate([along_re, along_im], axis=1), inverse_y)
    pre_act = spectral + conv_term + conv_bias[:, None, None]
    grad_pre = (cotangent[0].astype(jnp.float32) * gelu_slope(pre_act)).astype(jnp.bfloat16)
    back_spectra = forward_modes(grad_pre) * scale_modes
    sample_back = across_samples(back_spectra)
    gradient = jnp.sum(grad_term(sample_spectra, sample_back), axis=0)
    return gradient


def solution(mesh):
    return jax.shard_map(
        shards,
        mesh=mesh,
        in_specs=(
            P("dp", "mp", None, None, None),
            P("dp", "mp", None, None, None),
            P("dp", None, None, None, "mp"),
            P(),
            P(),
        ),
        out_specs=P("dp", None, None, None, "mp"),
        check_vma=False,
    )
```

profile of v0, /device:TPU:0, one launch (start us, length us, event | category | flops | bytes accessed | tf_op | source)
XLA Modules:
  0.0 728.4 jit_solution(3323887940892381672)
XLA Ops:
  0.3 13.5 %fusion.126 = f32[64,32,20,128]{3,0,2,1:T(8,128)} fusion(f32[128,32]{0,1:T(8,128)S(1)} %get-tuple-element.26, f32[128,32]{0,1:T(8,128)S(1)} %get-tuple-element.25, bf16[1,32,20,128,128]{4,3,2,1,0:T(8,128)(2,1)} %param.5), kind=kOutput, calls=%fused_computation.161 | convolution fusion | flops 1342218240 | bytes 41975808 | tf_op jit(solution)/shard_map/xcyz,yk->xckz/dot_general | solution.py:48
  13.8 13.5 %fusion.132 = f32[64,32,20,128]{3,0,2,1:T(8,128)} fusion(f32[128,32]{0,1:T(8,128)S(1)} %get-tuple-element.26, f32[128,32]{0,1:T(8,128)S(1)} %get-tuple-element.25, bf16[1,32,20,128,128]{4,3,2,1,0:T(8,128)(2,1)} %param.5), kind=kOutput, calls=%fused_computation.163 | convolution fusion | flops 1342210048 | bytes 41975808 | tf_op jit(solution)/shard_map/xcyz,yk->xckz/dot_general | solution.py:47
  27.2 66.3 %fusion.11 = f32[32,20,64,32]{2,3,1,0:T(8,128)} fusion(f32[64,32,20,128]{3,0,2,1:T(8,128)} %fusion.132, f32[64,32,20,128]{3,0,2,1:T(8,128)} %fusion.126, f32[128,16]{0,1:T(8,128)S(1)} %get-tuple-element.27, f32[128,16]{0,1:T(8,128)S(1)} %get-tuple-element.28), kind=kOutput, calls=%fused_computation.14 | convolution fusion | flops 2018512896 | bytes 47202304 | tf_op jit(solution)/shard_map/xckz,zm->xckm/dot_general | solution.py:105
  93.5 13.0 %fusion.23 = (f32[32,20,32,1,16]{2,4,1,0,3:T(8,128)}, f32[32,20,32,1,16]{2,4,1,0,3:T(8,128)}) fusion(f32[32,20,64,32]{2,3,1,0:T(8,128)} %fusion.11), kind=kLoop, calls=%fused_computation.36 | loop fusion | flops 655360 | bytes 7864320 | tf_op jit(solution)/shard_map/stack | solution.py:110
  106.5 4.9 maximum_bitcast_fusion
  111.4 5.4 copy.141
  116.8 7.0 copy.142
  123.8 65.6 %all_to_all.72 = f32[32,32,640]{2,0,1:T(8,128)S(1)} all-to-all(f32[32,32,640]{2,0,1:T(8,128)S(1)} %copy.142), channel_id=1, replica_groups=mesh['dp'=8,'mp'=4] {'mp'}, dimensions={1} | all-to-all | bytes 5242880 | tf_op jit(solution)/shard_map/all_to_all | solution.py:112
  217.3 4.5 copy.205
  235.0 4.8 fusion.38
  246.6 4.5 add_bitcast_fusion.1
  259.3 10.9 %all-to-all-done.2 = f32[8,4,5120]{2,1,0:T(4,128)S(1)} async-done(((f32[8,4,5120]{2,1,0:T(4,128)}), f32[8,4,5120]{2,1,0:T(4,128)S(1)}, u32[]{:S(2)}, u32[]{:S(2)}) %all-to-all-start.2) | async-done | bytes 655392 | tf_op jit(solution)/shard_map/all_to_all | solution.py:132
  287.0 31.1 %fusion.7 = f32[20,32,128,128]{3,0,2,1:T(8,128)} fusion(bf16[32,20,128,128]{3,2,1,0:T(8,128)(2,1)} %bitcast.238, bf16[20,20]{1,0:T(8,128)(2,1)S(1)} %copy-done), kind=kOutput, calls=%fused_computation.9 | convolution fusion | flops 419430400 | bytes 62915360 | tf_op jit(solution)/shard_map/xcyz,co->xoyz/dot_general | solution.py:129
  318.1 25.7 %all-to-all-done.3 = f32[128,8,640]{2,1,0:T(8,128)S(1)} async-done(((f32[128,8,640]{2,1,0:T(8,128)}), f32[128,8,640]{2,1,0:T(8,128)S(1)}, u32[]{:S(2)}, u32[]{:S(2)}) %all-to-all-start.3) | async-done | bytes 2621472 | tf_op jit(solution)/shard_map/all_to_all | solution.py:144
  345.6 8.8 %reshape.228 = f32[32,32,20,32]{3,2,1,0:T(8,128)} reshape(f32[32,4,8,640]{3,2,1,0:T(8,128)} %copy.164) | data formatting | bytes 5242880 | tf_op jit(solution)/shard_map/reshape | solution.py:144
  354.4 15.1 %fusion.16 = f32[32,32,20,128]{3,1,2,0:T(8,128)} fusion(f32[32,32,20,32]{3,2,1,0:T(8,128)} %reshape.228, f32[16,128]{1,0:T(8,128)S(1)} %get-tuple-element.24, f32[16,128]{1,0:T(8,128)S(1)} %get-tuple-element.23), kind=kOutput, calls=%fused_computation.23 | convolution fusion | flops 1006637056 | bytes 13123584 | tf_op jit(solution)/shard_map/xkcm,mz->xkcz/dot_general | solution.py:148
  369.5 10.7 %fusion.18 = f32[32,32,20,128]{3,1,2,0:T(8,128)} fusion(f32[32,32,20,32]{3,2,1,0:T(8,128)S(1)} %copy-done.2, f32[16,128]{1,0:T(8,128)S(1)} %broadcast_multiply_fusion.1, f32[16,128]{1,0:T(8,128)S(1)} %get-tuple-element.24), kind=kOutput, calls=%fused_computation.25 | convolution fusion | flops 1006637056 | bytes 13123584 | tf_op jit(solution)/shard_map/xkcm,mz->xkcz/dot_general | solution.py:147
  380.2 20.9 %fusion.45 = f32[128,32,20,128]{3,0,2,1:T(8,128)} fusion(f32[32,32,20,128]{3,1,2,0:T(8,128)} %fusion.16, f32[32,32,20,128]{3,1,2,0:T(8,128)} %fusion.18, f32[32,128]{1,0:T(8,128)S(1)} %get-tuple-element.22, f32[32,128]{1,0:T(8,128)S(1)} %get-tuple-element.21), kind=kOutput, calls=%fused_computation.60 | convolution fusion | flops 1363189760 | bytes 62947328 | tf_op jit(solution)/shard_map/xkcz,ky->xcyz/dot_general | solution.py:54
  401.1 21.0 %fusion.47 = f32[128,32,20,128]{3,0,2,1:T(8,128)} fusion(f32[32,32,20,128]{3,1,2,0:T(8,128)} %fusion.16, f32[32,32,20,128]{3,1,2,0:T(8,128)} %fusion.18, f32[32,128]{1,0:T(8,128)S(1)} %get-tuple-element.22, f32[32,128]{1,0:T(8,128)S(1)} %get-tuple-element.21), kind=kOutput, calls=%fused_computation.61 | convolution fusion | flops 1363181568 | bytes 62947328 | tf_op jit(solution)/shard_map/xkcz,ky->xcyz/dot_general | solution.py:53
  422.0 63.2 %fusion.5 = bf16[32,20,128,128]{3,2,1,0:T(8,128)(2,1)} fusion(f32[20,32,128,128]{3,0,2,1:T(8,128)} %fusion.7, f32[128,32,20,128]{3,0,2,1:T(8,128)} %fusion.47, f32[128,32,20,128]{3,0,2,1:T(8,128)} %fusion.45, bf16[1,32,20,128,128]{4,3,2,1,0:T(8,128)(2,1)} %param.6, f32[20]{0:T(128)S(1)} %copy-done.21, f32[32,32,20,128]{3,1,2,0:T(8,128)} %fusion.16, ...), kind=kOutput, calls=%fused_computation.6 | convolution fusion | flops 1525710848 | bytes 188776528 | tf_op jit(solution)/shard_map/xkcz,ky->xcyz/dot_general | solution.py:55
  485.2 13.5 %fusion.124 = f32[64,32,20,128]{3,0,2,1:T(8,128)} fusion(bf16[32,20,128,128]{3,2,1,0:T(8,128)(2,1)} %fusion.5, f32[128,32]{0,1:T(8,128)S(1)} %copy-done.12, f32[128,32]{0,1:T(8,128)S(1)} %copy-done.10), kind=kOutput, calls=%fused_computation.160 | convolution fusion | flops 1342218240 | bytes 41975808 | tf_op jit(solution)/shard_map/xcyz,yk->xckz/dot_general | solution.py:48
  498.7 13.5 %fusion.130 = f32[64,32,20,128]{3,0,2,1:T(8,128)} fusion(bf16[32,20,128,128]{3,2,1,0:T(8,128)(2,1)} %fusion.5, f32[128,32]{0,1:T(8,128)S(1)} %copy-done.12, f32[128,32]{0,1:T(8,128)S(1)} %copy-done.10), kind=kOutput, calls=%fused_computation.162 | convolution fusion | flops 1342210048 | bytes 41975808 | tf_op jit(solution)/shard_map/xcyz,yk->xckz/dot_general | solution.py:47
  512.2 66.6 %fusion.9 = f32[32,20,64,32]{2,3,1,0:T(8,128)} fusion(f32[64,32,20,128]{3,0,2,1:T(8,128)} %fusion.130, f32[64,32,20,128]{3,0,2,1:T(8,128)} %fusion.124, f32[128,16]{0,1:T(8,128)S(1)} %copy-done.14, f32[128,16]{0,1:T(8,128)S(1)} %copy-done.16), kind=kOutput, calls=%fused_computation.12 | convolution fusion | flops 2018512896 | bytes 47202304 | tf_op jit(solution)/shard_map/xckz,zm->xckm/dot_general | solution.py:105
  578.8 12.8 %fusion.21 = (f32[32,20,32,1,16]{2,4,1,0,3:T(8,128)}, f32[32,20,32,1,16]{2,4,1,0,3:T(8,128)}) fusion(f32[32,20,64,32]{2,3,1,0:T(8,128)} %fusion.9), kind=kLoop, calls=%fused_computation.32 | loop fusion | flops 655360 | bytes 7864320 | tf_op jit(solution)/shard_map/stack | solution.py:110
  591.6 4.9 maximum_bitcast_fusion.1
  596.5 5.4 copy.170
  601.9 8.4 %copy.171 = f32[32,32,640]{2,0,1:T(8,128)} copy(f32[32,32,640]{1,2,0:T(8,128)} %bitcast.240) | data formatting | bytes 5242880 | tf_op jit(solution)/shard_map/reshape | solution.py:111
  614.2 58.7 %all-to-all-done.4 = f32[32,32,640]{2,0,1:T(8,128)S(1)} async-done(((f32[32,32,640]{2,0,1:T(8,128)}), f32[32,32,640]{2,0,1:T(8,128)S(1)}, u32[]{:S(2)}, u32[]{:S(2)}) %all-to-all-start.4) | async-done | bytes 2621472 | tf_op jit(solution)/shard_map/all_to_all | solution.py:112
  692.7 5.0 all-to-all-start.5
  698.2 10.7 %all-to-all-done.5 = f32[1,32,5120]{2,0,1:T(1,128)S(1)} async-done(((f32[1,32,5120]{2,0,1:T(1,128)}), f32[1,32,5120]{2,0,1:T(1,128)S(1)}, u32[]{:S(2)}, u32[]{:S(2)}) %all-to-all-start.5) | async-done | bytes 655392 | tf_op jit(solution)/shard_map/all_to_all | solution.py:122
  711.1 6.7 add_bitcast_fusion
  717.8 8.0 %maximum_reduce_fusion = f32[4,2,20,20,128]{4,3,2,1,0:T(8,128)S(1)} fusion(f32[8,4,1,20,20,128]{5,0,4,3,2,1:T(8,128)} %get-tuple-element.12, f32[8,4,1,20,20,128]{5,0,4,3,2,1:T(8,128)} %get-tuple-element.11), kind=kLoop, calls=%fused_computation.20 | loop fusion | flops 6144000 | bytes 14745600 | tf_op jit(solution)/shard_map/reduce_sum | solution.py:154
  (112 shorter events, 103.3 us)
Async XLA Ops:
  0.0 287.0 %copy-start = (bf16[20,20]{1,0:T(8,128)(2,1)S(1)}, bf16[20,20]{1,0:T(8,128)(2,1)}, u32[]{:S(2)}) copy-start(bf16[20,20]{1,0:T(8,128)(2,1)} %param.8) | copy-start | bytes 2404
  0.0 275.5 %copy-start.17 = (s32[32]{0:T(128)}, s32[32]{0:T(128)S(1)}, u32[]{:S(2)}) copy-start(s32[32]{0:T(128)S(1)} %compare_select_fusion) | copy-start | bytes 388
  0.1 27.2 %copy-start.13 = (f32[128,16]{0,1:T(8,128)}, f32[128,16]{0,1:T(8,128)S(1)}, u32[]{:S(2)}) copy-start(f32[128,16]{0,1:T(8,128)S(1)} %get-tuple-element.27) | copy-start | bytes 24580
  0.1 27.2 %copy-start.15 = (f32[128,16]{0,1:T(8,128)}, f32[128,16]{0,1:T(8,128)S(1)}, u32[]{:S(2)}) copy-start(f32[128,16]{0,1:T(8,128)S(1)} %get-tuple-element.28) | copy-start | bytes 24580
  0.2 13.5 %copy-start.9 = (f32[128,32]{0,1:T(8,128)}, f32[128,32]{0,1:T(8,128)S(1)}, u32[]{:S(2)}) copy-start(f32[128,32]{0,1:T(8,128)S(1)} %get-tuple-element.25) | copy-start | bytes 49156
  0.3 13.5 %copy-start.11 = (f32[128,32]{0,1:T(8,128)}, f32[128,32]{0,1:T(8,128)S(1)}, u32[]{:S(2)}) copy-start(f32[128,32]{0,1:T(8,128)S(1)} %get-tuple-element.26) | copy-start | bytes 49156
  203.9 7.2 copy-start.6
  206.9 15.4 %all-to-all-start.1 = ((f32[1,32,5120]{2,0,1:T(1,128)}), f32[1,32,5120]{2,0,1:T(1,128)}, u32[]{:S(2)}, u32[]{:S(2)}) async-start(f32[1,32,5120]{2,0,1:T(1,128)} %copy.151), calls=%async_computation.1 | async-start | bytes 1310720 | tf_op jit(solution)/shard_map/all_to_all | solution.py:122
  235.0 4.8 copy-start.5
  239.8 3.1 copy-start.3
  243.0 3.6 copy-start.4
  255.3 14.9 %all-to-all-start.2 = ((f32[8,4,5120]{2,1,0:T(4,128)}), f32[8,4,5120]{2,1,0:T(4,128)S(1)}, u32[]{:S(2)}, u32[]{:S(2)}) async-start(f32[8,4,5120]{2,1,0:T(4,128)} %copy.158), calls=%async_computation.2 | async-start | bytes 1310720 | tf_op jit(solution)/shard_map/all_to_all | solution.py:132
  259.1 16.4 %copy-start.19 = (f32[16]{0:T(128)}, f32[16]{0:T(128)S(1)}, u32[]{:S(2)}) copy-start(f32[16]{0:T(128)S(1)} %fusion.134) | copy-start | bytes 196
  283.1 60.7 %all-to-all-start.3 = ((f32[128,8,640]{2,1,0:T(8,128)}), f32[128,8,640]{2,1,0:T(8,128)S(1)}, u32[]{:S(2)}, u32[]{:S(2)}) async-start(f32[128,8,640]{2,1,0:T(8,128)} %copy.163), calls=%async_computation.3 | async-start | bytes 5242880 | tf_op jit(solution)/shard_map/all_to_all | solution.py:144
  354.4 15.1 %copy-start.2 = (f32[32,32,20,32]{3,2,1,0:T(8,128)S(1)}, f32[32,32,20,32]{3,2,1,0:T(8,128)}, u32[]{:S(2)}) copy-start(f32[32,32,20,32]{3,2,1,0:T(8,128)} %reshape.228) | copy-start | bytes 7864324
  401.1 21.0 %copy-start.21 = (f32[20]{0:T(128)S(1)}, f32[20]{0:T(128)}, u32[]{:S(2)}) copy-start(f32[20]{0:T(128)} %param.9) | copy-start | bytes 244
  422.0 63.2 %copy-start.10 = (f32[128,32]{0,1:T(8,128)S(1)}, f32[128,32]{0,1:T(8,128)}, u32[]{:S(2)}) copy-start(f32[128,32]{0,1:T(8,128)} %copy-done.9) | copy-start | bytes 49156
  422.0 63.2 %copy-start.12 = (f32[128,32]{0,1:T(8,128)S(1)}, f32[128,32]{0,1:T(8,128)}, u32[]{:S(2)}) copy-start(f32[128,32]{0,1:T(8,128)} %copy-done.11) | copy-start | bytes 49156
  498.7 13.5 %copy-start.14 = (f32[128,16]{0,1:T(8,128)S(1)}, f32[128,16]{0,1:T(8,128)}, u32[]{:S(2)}) copy-start(f32[128,16]{0,1:T(8,128)} %copy-done.13) | copy-start | bytes 24580
  498.7 13.5 %copy-start.16 = (f32[128,16]{0,1:T(8,128)S(1)}, f32[128,16]{0,1:T(8,128)}, u32[]{:S(2)}) copy-start(f32[128,16]{0,1:T(8,128)} %copy-done.15) | copy-start | bytes 24580
  610.3 3.8 copy-start.20
  610.3 62.6 %all-to-all-start.4 = ((f32[32,32,640]{2,0,1:T(8,128)}), f32[32,32,640]{2,0,1:T(8,128)S(1)}, u32[]{:S(2)}, u32[]{:S(2)}) async-start(f32[32,32,640]{2,0,1:T(8,128)} %copy.171), calls=%async_computation.4 | async-start | bytes 5242880 | tf_op jit(solution)/shard_map/all_to_all | solution.py:112
  674.4 4.1 copy-start.18
  687.9 9.9 %copy-start.8 = (f32[8,4,128,20]{2,3,1,0:T(8,128)S(1)}, f32[8,4,128,20]{2,3,1,0:T(8,128)}, u32[]{:S(2)}) copy-start(f32[8,4,128,20]{2,3,1,0:T(8,128)} %get-tuple-element.17) | copy-start | bytes 983044
  687.9 10.1 %copy-start.7 = (f32[8,4,128,20]{2,3,1,0:T(8,128)S(1)}, f32[8,4,128,20]{2,3,1,0:T(8,128)}, u32[]{:S(2)}) copy-start(f32[8,4,128,20]{2,3,1,0:T(8,128)} %get-tuple-element.18) | copy-start | bytes 983044
  692.7 16.2 %all-to-all-start.5 = ((f32[1,32,5120]{2,0,1:T(1,128)}), f32[1,32,5120]{2,0,1:T(1,128)S(1)}, u32[]{:S(2)}, u32[]{:S(2)}) async-start(f32[1,32,5120]{2,0,1:T(1,128)} %copy.180), calls=%async_computation.5 | async-start | bytes 1310720 | tf_op jit(solution)/shard_map/all_to_all | solution.py:122
  717.8 10.4 %copy-start.1 = (bf16[20,20]{1,0:T(8,128)(2,1)S(1)}, bf16[20,20]{1,0:T(8,128)(2,1)}, u32[]{:S(2)}) copy-start(bf16[20,20]{1,0:T(8,128)(2,1)} %param.8) | copy-start | bytes 2404
where the time goes:
time: 733 us; the launch traced here: 728 us
  matrix products  389 us (53%)
  waiting for transfers between devices  106 us (14%)
  local copies, waits for them, and re-layouts  85.6 us (12%)
  blocking collectives  65.6 us (9%)
  other arithmetic  60.2 us (8%)
  starting transfers between devices  20.5 us (3%)
    dot_general x2, matrix products, forward_modes(): along_yz = jnp.einsum('xckz,zm->xckm', along_y, table_z, precision=highest)  133 us
    all_to_all x1, blocking collectives, forward_modes(): lax.all_to_all(packed, 'mp', split_axis=1, concat_axis=0, tiled=True)  65.6 us
    dot_general x1, matrix products, three_pass(): jnp.einsum(form, data_lo, table_pair[0], preferred_element_type=jnp.float32)  63.2 us
    all_to_all x1, waiting for transfers between devices, forward_modes(): lax.all_to_all(packed, 'mp', split_axis=1, concat_axis=0, tiled=True)  58.7 us
    dot_general x1, matrix products, shards(): jnp.einsum('xcyz,co->xoyz', volume, conv_weight, preferred_element_type=j...  31.1 us
    dot_general x2, matrix products, two_pass(): jnp.einsum(form, data_bf, table_pair[1], preferred_element_type=jnp.float32)  27 us
    dot_general x2, matrix products, two_pass(): jnp.einsum(form, data_bf, table_pair[0], preferred_element_type=jnp.float32)  27 us
    another operation x2, other arithmetic, forward_modes(): packed = jnp.stack([a_cos - b_sin, b_cos + a_sin], axis=3)  25.8 us
  transfers between devices with their start and end apart: 5, of which 5 were waited for; matrix products, arithmetic and copies ran while one was open for 6% of the time, Pallas kernels for 0%

commit v1 on v0

v1 whole, which is shorter than its diff:
```python
import functools
import math

import jax
import jax.numpy as jnp
import ml_dtypes
import numpy as np
from jax import lax
from jax.experimental import pallas as pl
from jax.experimental.pallas import tpu as pltpu
from jax.sharding import PartitionSpec as P

KX = 32
KY = 32
KZ = 16
ROWS = 16
VMEM_BYTES = 50 * 2**20

f32 = jnp.float32
bf16 = jnp.bfloat16


def kept_modes(count, length):
    indices = np.arange(count)
    return np.where(indices < count // 2, indices, length - count + indices)


def rounded(values):
    return np.asarray(values, np.float32).astype(ml_dtypes.bfloat16)


def split_parts(values):
    upper = rounded(values)
    return upper, rounded(values - upper.astype(np.float64))


def make_tables(x_cells, y_cells, z_cells, slabs):
    slab_len = x_cells // slabs
    kx = kept_modes(KX, x_cells)
    kx = np.where(kx >= x_cells // 2, kx - x_cells, kx)
    part = np.exp(-2j * math.pi * np.outer(kx, np.arange(slab_len)) / x_cells)
    left, scale, right = np.linalg.svd(part, full_matrices=False)
    rank = int(np.sum(scale > scale[0] * np.finfo(np.float32).eps))
    rank = min(rank + rank % 2, slab_len)
    left = left[:, :rank] * scale[:rank]
    right = right[:rank]
    shifts = np.exp(-2j * math.pi * np.outer(kx, np.arange(slabs) * slab_len) / x_cells)
    outer = shifts[:, :, None] * left[:, None, :]
    table_x = np.zeros((KX, 2, slabs, rank, 2))
    table_x[:, 0, :, :, 0] = outer.real
    table_x[:, 0, :, :, 1] = -outer.imag
    table_x[:, 1, :, :, 0] = outer.imag
    table_x[:, 1, :, :, 1] = outer.real
    table_x = table_x.reshape(KX * 2, slabs * rank * 2)
    wave_z = np.exp(-2j * math.pi * np.outer(np.arange(z_cells), np.arange(KZ)) / z_cells)
    inner = right.T[:, None, :, None] * wave_z[None, :, None, :]
    table_zx = np.zeros((slab_len, 2, z_cells, rank, 2, KZ))
    table_zx[:, 0, :, :, 0] = inner.real
    table_zx[:, 1, :, :, 0] = -inner.imag
    table_zx[:, 0, :, :, 1] = inner.imag
    table_zx[:, 1, :, :, 1] = inner.real
    table_zx = table_zx.reshape(slab_len, 2 * z_cells, rank * 2 * KZ)
    phase_y = 2.0 * math.pi * np.outer(kept_modes(KY, y_cells), np.arange(y_cells)) / y_cells
    table_y = np.concatenate([np.cos(phase_y), -np.sin(phase_y)], axis=0)
    return rank, table_x, table_zx, table_y


def dot(left, right, contract=((1,), (0,))):
    return lax.dot_general(left, right, (contract, ((), ())), preferred_element_type=f32)


def y_modes(pair, table, modes_ref, channel, z_cells):
    both = dot(table, pair)
    half = 2 * KY
    total = both[:half] + both[half:]
    for i in range(2):
        one = total[:, i * z_cells : (i + 1) * z_cells].astype(bf16)
        rows = pl.ds((channel + i) * KY, KY)
        modes_ref[rows, :z_cells] = one[:KY]
        modes_ref[rows, z_cells:] = one[KY:]


def forward_kernel(fields_ref, table_y_ref, table_zx_ref, out_ref, modes_ref, total_ref):
    channels, _, z_cells = fields_ref.shape[1:]
    step = pl.program_id(0)
    table = table_y_ref[...]
    for c in range(0, channels, 2):
        pair = jnp.concatenate([fields_ref[0, c], fields_ref[0, c + 1]], axis=1)
        y_modes(pair, table, modes_ref, c, z_cells)
    term = dot(modes_ref[...], table_zx_ref[0])

    @pl.when(step == 0)
    def _():
        total_ref[...] = term

    @pl.when(step > 0)
    def _():
        total_ref[...] += term

    @pl.when(step == pl.num_programs(0) - 1)
    def _():
        out_ref[...] = total_ref[...].astype(bf16)


def gelu_slope(values):
    size = jnp.abs(values)
    bell = jnp.exp(values * values * -0.5)
    base = 1.0 + size * (0.3275911 * math.sqrt(0.5))
    t = pl.reciprocal(base, approx=True)
    t = t * (2.0 - base * t)
    tail = t * (
        0.5 * 0.254829592
        + t * (0.5 * -0.284496736 + t * (0.5 * 1.421413741 + t * (0.5 * -1.453152027 + t * (0.5 * 1.061405429))))
    )
    part = bell * (size * 0.3989422804014327 - tail)
    return jnp.where(values >= 0.0, 1.0 + part, -part)


def slope_kernel(
    bias_ref,
    fields_ref,
    cotangent_ref,
    mixed_ref,
    conv_ref,
    table_y_ref,
    inverse_y_ref,
    table_zx_ref,
    out_ref,
    back_ref,
    pre_ref,
    modes_ref,
    total_ref,
):
    channels, y_cells, z_cells = fields_ref.shape[1:]
    step = pl.program_id(0)
    table = table_y_ref[...]
    inverse_y = inverse_y_ref[...]
    mixing = conv_ref[...]
    back_ref[...] = dot(mixed_ref[...], table_zx_ref[0], ((1,), (1,))).astype(bf16)
    for g in range(0, y_cells, 2 * ROWS):
        pair = jnp.concatenate(
            [
                fields_ref[0, :, g : g + ROWS, :].reshape(channels * ROWS, z_cells),
                fields_ref[0, :, g + ROWS : g + 2 * ROWS, :].reshape(channels * ROWS, z_cells),
            ],
            axis=1,
        )
        conv = dot(mixing, pair)
        pre_ref[:, g : g + ROWS, :] = conv[:, :z_cells].reshape(channels, ROWS, z_cells)
        pre_ref[:, g + ROWS : g + 2 * ROWS, :] = conv[:, z_cells:].reshape(channels, ROWS, z_cells)
    for o in range(0, channels, 2):
        columns = []
        for i in range(2):
            one = back_ref[(o + i) * KY : (o + i + 1) * KY, :]
            columns.append(jnp.concatenate([one[:, :z_cells], one[:, z_cells:]], axis=0))
        spectral = dot(inverse_y, jnp.concatenate(columns, axis=1))
        deltas = []
        for i in range(2):
            pre = spectral[:, i * z_cells : (i + 1) * z_cells] + pre_ref[o + i] + bias_ref[o + i]
            deltas.append((cotangent_ref[0, o + i].astype(f32) * gelu_slope(pre)).astype(bf16))
        y_modes(jnp.concatenate(deltas, axis=1), table, modes_ref, o, z_cells)
    term = dot(modes_ref[...], table_zx_ref[0])

    @pl.when(step == 0)
    def _():
        total_ref[...] = term

    @pl.when(step > 0)
    def _():
        total_ref[...] += term

    @pl.when(step == pl.num_programs(0) - 1)
    def _():
        out_ref[...] = total_ref[...].astype(bf16)


def mix_kernel(spectra_ref, weight_ref, scale_ref, out_ref):
    samples, _, _, channels, _ = spectra_ref.shape
    scale = scale_ref[...]

    def one_sample(s, carry):
        real = jnp.zeros(out_ref.shape[3:], f32)
        imag = jnp.zeros(out_ref.shape[3:], f32)
        spec_re = spectra_ref[s, 0, 0].astype(f32) * scale
        spec_im = spectra_ref[s, 0, 1].astype(f32) * scale
        for c in range(channels):
            real_w = weight_ref[0, 0, c].astype(f32)
            imag_w = weight_ref[0, 1, c].astype(f32)
            real += spec_re[c : c + 1] * real_w - spec_im[c : c + 1] * imag_w
            imag += spec_re[c : c + 1] * imag_w + spec_im[c : c + 1] * real_w
        out_ref[s, 0, 0] = real.astype(out_ref.dtype)
        out_ref[s, 0, 1] = imag.astype(out_ref.dtype)
        return carry

    lax.fori_loop(0, samples, one_sample, 0)


def grad_kernel(spectra_ref, back_ref, scale_ref, out_ref):
    samples, _, _, channels, _ = spectra_ref.shape
    scale = scale_ref[...]
    for c in range(channels):
        real = jnp.zeros(out_ref.shape[3:], f32)
        imag = jnp.zeros(out_ref.shape[3:], f32)
        for s in range(samples):
            spec_re = spectra_ref[s, 0, 0, c : c + 1].astype(f32)
            spec_im = spectra_ref[s, 0, 1, c : c + 1].astype(f32)
            back_re = back_ref[s, 0, 0].astype(f32)
            back_im = back_ref[s, 0, 1].astype(f32)
            real += spec_re * back_re + spec_im * back_im
            imag += spec_re * back_im - spec_im * back_re
        out_ref[0, 0, c] = real * scale
        out_ref[0, 1, c] = imag * scale


def shards(fields, cotangent, spectral_weight, conv_weight, conv_bias):
    _, slab_len, channels, y_cells, z_cells = fields.shape
    slabs = lax.axis_size("mp")
    data_count = lax.axis_size("dp")
    kx_local = spectral_weight.shape[0]
    ky_local = KY // slabs
    x_cells = slab_len * slabs
    rank, table_x, table_zx, table_y = make_tables(x_cells, y_cells, z_cells, slabs)
    lanes = rank * 2 * KZ
    table_x = jnp.asarray(table_x.astype(np.float32))
    table_zx = jnp.asarray(rounded(table_zx))
    y_parts = jnp.asarray(np.concatenate(split_parts(table_y), axis=0))
    inverse_y = jnp.asarray(rounded(table_y.T))
    weight_z = np.where(np.arange(KZ) == 0, 1.0, 2.0) / (x_cells * y_cells * z_cells)
    scale = jnp.asarray(np.tile(weight_z, ky_local)[None].astype(np.float32))
    mixing = jnp.kron(conv_weight.T, jnp.eye(ROWS, dtype=bf16))
    mode_cells = ky_local * KZ

    cell_spec = pl.BlockSpec((1, channels, y_cells, z_cells), lambda x: (x, 0, 0, 0))
    zx_spec = pl.BlockSpec((1, 2 * z_cells, lanes), lambda x: (x, 0, 0))

    def whole(shape):
        return pl.BlockSpec(shape, lambda x: (0,) * len(shape))

    params = pltpu.CompilerParams(
        dimension_semantics=("arbitrary",), vmem_limit_bytes=VMEM_BYTES
    )
    coefs_shape = (channels * KY, lanes)
    coefs_out = jax.ShapeDtypeStruct(coefs_shape, bf16)
    work = [
        pltpu.VMEM((channels * KY, 2 * z_cells), bf16),
        pltpu.VMEM(coefs_shape, f32),
    ]

    def to_modes(coefs):
        packed = coefs.reshape(channels, slabs, ky_local, rank * 2, KZ)
        packed = jnp.transpose(packed, (1, 3, 0, 2, 4)).reshape(slabs, rank * 2, -1)
        moved = lax.all_to_all(packed, "mp", split_axis=0, concat_axis=0, tiled=True)
        moved = moved.reshape(slabs * rank * 2, -1).astype(f32)
        return jnp.dot(table_x, moved, precision=lax.Precision.HIGHEST)

    def across_samples(modes):
        modes = modes.reshape(data_count, kx_local * 2, -1)
        moved = lax.all_to_all(modes, "dp", split_axis=0, concat_axis=0, tiled=True)
        return moved.reshape(data_count, kx_local, 2, channels, mode_cells)

    with jax.named_scope("forward_fields"):
        coefs = pl.pallas_call(
            forward_kernel,
            grid=(slab_len,),
            in_specs=[cell_spec, whole(y_parts.shape), zx_spec],
            out_specs=whole(coefs_shape),
            out_shape=coefs_out,
            scratch_shapes=work,
            compiler_params=params,
        )(fields[0], y_parts, table_zx)
    sample_spectra = across_samples(to_modes(coefs))

    sample_spec = pl.BlockSpec(
        (data_count, 1, 2, channels, mode_cells), lambda k: (0, k, 0, 0, 0)
    )
    weight_spec = pl.BlockSpec(
        (1, 2, channels, channels, mode_cells), lambda k: (k, 0, 0, 0, 0)
    )
    with jax.named_scope("mix_modes"):
        local_mixed = pl.pallas_call(
            mix_kernel,
            grid=(kx_local,),
            in_specs=[sample_spec, weight_spec, whole(scale.shape)],
            out_specs=sample_spec,
            out_shape=jax.ShapeDtypeStruct(sample_spectra.shape, bf16),
            compiler_params=params,
        )(sample_spectra, spectral_weight, scale)
    returned = lax.all_to_all(
        local_mixed.reshape(data_count, kx_local * 2, -1),
        "dp",
        split_axis=0,
        concat_axis=0,
        tiled=True,
    )
    mixed = returned.reshape(KX * 2, -1).astype(f32)
    slab_mixed = jnp.dot(table_x.T, mixed, precision=lax.Precision.HIGHEST).astype(bf16)
    moved = lax.all_to_all(
        slab_mixed.reshape(slabs, rank * 2, -1), "mp", split_axis=0, concat_axis=0, tiled=True
    )
    moved = moved.reshape(slabs, rank * 2, channels, ky_local, KZ)
    mixed_coefs = jnp.transpose(moved, (2, 0, 3, 1, 4)).reshape(coefs_shape)

    with jax.named_scope("slope_and_back"):
        back_coefs = pl.pallas_call(
            slope_kernel,
            grid=(slab_len,),
            in_specs=[
                pl.BlockSpec(memory_space=pltpu.SMEM),
                cell_spec,
                cell_spec,
                whole(coefs_shape),
                whole(mixing.shape),
                whole(y_parts.shape),
                whole(inverse_y.shape),
                zx_spec,
            ],
            out_specs=whole(coefs_shape),
            out_shape=coefs_out,
            scratch_shapes=[
                pltpu.VMEM((channels * KY, 2 * z_cells), bf16),
                pltpu.VMEM((channels, y_cells, z_cells), f32),
            ]
            + work,
            compiler_params=params,
        )(conv_bias, fields[0], cotangent[0], mixed_coefs, mixing, y_parts, inverse_y, table_zx)
    sample_back = across_samples(to_modes(back_coefs))

    with jax.named_scope("weight_gradient"):
        return pl.pallas_call(
            grad_kernel,
            grid=(kx_local,),
            in_specs=[sample_spec, sample_spec, whole(scale.shape)],
            out_specs=weight_spec,
            out_shape=jax.ShapeDtypeStruct(spectral_weight.shape, f32),
            compiler_params=params,
        )(sample_spectra, sample_back, scale)


def solution(mesh):
    return jax.shard_map(
        shards,
        mesh=mesh,
        in_specs=(
            P("dp", "mp", None, None, None),
            P("dp", "mp", None, None, None),
            P("dp", None, None, None, "mp"),
            P(),
            P(),
        ),
        out_specs=P("dp", None, None, None, "mp"),
        check_vma=False,
    )
```

time: 733 us -> 319 us (0.44)
  matrix products: 389 us -> 2.51 us
  Pallas kernels: 0 us -> 143 us
  waiting for transfers between devices: 106 us -> 30.4 us
  other arithmetic: 60.2 us -> 0.2 us
  local copies, waits for them, and re-layouts: 85.6 us -> 57.5 us
  starting transfers between devices: 20.5 us -> 8.23 us
  blocking collectives: 65.6 us -> 74.6 us
    dot_general x22 -> x3, matrix products: 389 us -> 2.51 us  [the longest x2 1.73 us: to_modes(): return jnp.dot(table_x, moved, precision=lax.Precision.HIGHEST)]
    pallas_call x0 -> x4, Pallas kernels: none -> 143 us  [the longest x1 104 us: shards(): pl.pallas_call(slope_kernel, grid=(slab_len,), in_specs=[pl.BlockSpec(mem...]
    all_to_all x5 -> x2, waiting for transfers between devices: 106 us -> 30.4 us  [the longest x1 19.4 us: shards(): lax.all_to_all(slab_mixed.reshape(slabs, rank * 2, -1), 'mp', split_axis=...]
    another operation x4 -> x0, other arithmetic: 32.5 us -> none  [the longest x2 25.8 us: forward_modes(): packed = jnp.stack([a_cos - b_sin, b_cos + a_sin], axis=3)]
    unnamed x50 -> x17, local copies, waits for them, and re-layouts: 17.7 us -> 0.92 us
    all_to_all x5 -> x2, starting transfers between devices: 20.5 us -> 8.23 us  [the longest x1 4.38 us: shards(): lax.all_to_all(slab_mixed.reshape(slabs, rank * 2, -1), 'mp', split_axis=...]
    transpose x5 -> x4, local copies, waits for them, and re-layouts: 12.3 us -> 23.5 us  [the longest x2 15.2 us: to_modes(): packed = jnp.transpose(packed, (1, 3, 0, 2, 4)).reshape(slabs, rank * 2, -1)]
    transpose x5 -> x0, other arithmetic: 10.6 us -> none  [the longest x2 9.81 us: forward_modes(): packed = jnp.transpose(packed, (0, 2, 1, 3, 4)).reshape(slab_len, KY, -1)]
  transfers between devices with their start and end apart: 5 -> 2, of which waited for: 5 -> 2; matrix products, arithmetic and copies ran while one was open for 6% -> 1% of each run, Pallas kernels for 0% -> 0%
where the time goes in v1:
time: 319 us; the launch traced here: 317 us
  Pallas kernels  143 us (45%)
  blocking collectives  74.6 us (23%)
  local copies, waits for them, and re-layouts  57.5 us (18%)
  waiting for transfers between devices  30.4 us (10%)
  starting transfers between devices  8.23 us (3%)
    pallas_call x1, Pallas kernels, shards(): pl.pallas_call(slope_kernel, grid=(slab_len,), in_specs=[pl.BlockSpec(mem...  104 us
    all_to_all x2, blocking collectives, to_modes(): lax.all_to_all(packed, 'mp', split_axis=0, concat_axis=0, tiled=True)  51.1 us
    pallas_call x1, Pallas kernels, shards(): pl.pallas_call(forward_kernel, grid=(slab_len,), in_specs=[cell_spec, who...  33.6 us
    all_to_all x1, waiting for transfers between devices, shards(): lax.all_to_all(slab_mixed.reshape(slabs, rank * 2, -1), 'mp', split_axis=...  19.4 us
    transpose x2, local copies, waits for them, and re-layouts, to_modes(): packed = jnp.transpose(packed, (1, 3, 0, 2, 4)).reshape(slabs, rank * 2, -1)  15.2 us
    all_to_all x1, blocking collectives, across_samples(): moved = lax.all_to_all(modes, 'dp', split_axis=0, concat_axis=0, tiled=True)  13.5 us
    reshape x2, local copies, waits for them, and re-layouts, to_modes(): packed = coefs.reshape(channels, slabs, ky_local, rank * 2, KZ)  11.5 us
    all_to_all x1, waiting for transfers between devices, across_samples(): moved = lax.all_to_all(modes, 'dp', split_axis=0, concat_axis=0, tiled=True)  11 us
  transfers between devices with their start and end apart: 2, of which 2 were waited for; matrix products, arithmetic and copies ran while one was open for 1% of the time, Pallas kernels for 0%

profile of v1, /device:TPU:0, one launch (start us, length us, event | category | flops | bytes accessed | tf_op | source)
XLA Modules:
  0.0 317.0 jit_solution(10738820428645251255)
XLA Ops:
  0.0 0.8 copy-done
  0.8 33.6 %forward_fields.1 = bf16[640,576]{1,0:T(8,128)(2,1)S(1)} custom-call(bf16[32,20,128,128]{3,2,1,0:T(8,128)(2,1)} %bitcast.24, bf16[128,128]{1,0:T(8,128)(2,1)S(1)} %copy-done, bf16[32,256,576]{2,1,0:T(8,128)(2,1)} %constant.11.clone.table_zx_ref), custom_call_target="tpu_custom_call" | custom-call | tf_op jit(solution)/shard_map/forward_fields/pallas_call | solution.py:262
  34.4 5.8 %reshape.59 = bf16[20,4,8,36,16]{4,3,2,1,0:T(8,128)(2,1)} reshape(bf16[640,576]{1,0:T(8,128)(2,1)S(1)} %forward_fields.1) | data formatting | bytes 1474560 | tf_op jit(solution)/shard_map/reshape | solution.py:250
  40.1 7.6 %copy.23 = bf16[4,36,20,8,16]{1,4,3,2,0:T(8,128)(2,1)S(1)} copy(bf16[4,36,20,8,16]{4,1,3,0,2:T(8,128)(2,1)} %bitcast.26) | data formatting | bytes 1474560 | tf_op jit(solution)/shard_map/transpose | solution.py:251
  47.8 2.6 copy.24
  50.3 27.3 %all_to_all.30 = bf16[4,36,2560]{2,1,0:T(8,128)(2,1)S(1)} all-to-all(bf16[4,36,2560]{2,1,0:T(8,128)(2,1)} %copy.24), channel_id=1, replica_groups=mesh['dp'=8,'mp'=4] {'mp'}, dimensions={0} | all-to-all | bytes 1474560 | tf_op jit(solution)/shard_map/all_to_all | solution.py:252
  77.6 0.1 reshape.61
  77.7 1.3 convolution_bitcast_fusion.1
  79.0 3.9 %all-to-all-start.1 = ((f32[8,8,2560]{2,1,0:T(8,128)}), f32[8,8,2560]{2,1,0:T(8,128)S(1)}, u32[]{:S(2)}, u32[]{:S(2)}) async-start(f32[8,8,2560]{2,1,0:T(8,128)} %convolution_bitcast_fusion.1), calls=%async_computation.1 | async-start | bytes 1310720 | tf_op jit(solution)/shard_map/all_to_all | solution.py:258
  83.0 11.0 %all-to-all-done.1 = f32[8,8,2560]{2,1,0:T(8,128)S(1)} async-done(((f32[8,8,2560]{2,1,0:T(8,128)}), f32[8,8,2560]{2,1,0:T(8,128)S(1)}, u32[]{:S(2)}, u32[]{:S(2)}) %all-to-all-start.1) | async-done | bytes 655392 | tf_op jit(solution)/shard_map/all_to_all | solution.py:258
  94.1 3.8 %mix_modes.1 = bf16[8,4,2,20,128]{4,3,2,1,0:T(8,128)(2,1)S(1)} custom-call(f32[8,4,2,20,128]{4,3,2,1,0:T(8,128)S(1)} %reshape.63.spectra_ref, bf16[4,2,20,20,128]{4,3,2,1,0:T(8,128)(2,1)S(1)} %copy.25.weight_ref, f32[1,128]{1,0:T(1,128)S(1)} %copy-done.3), custom_call_target="tpu_custom_call" | custom-call | tf_op jit(solution)/shard_map/mix_modes/pallas_call | solution.py:280
  98.0 0.2 reshape.64
  98.2 10.0 %all_to_all.31 = bf16[8,8,2560]{2,1,0:T(8,128)(2,1)S(1)} all-to-all(bf16[8,8,2560]{2,1,0:T(8,128)(2,1)S(1)} %reshape.64), channel_id=1, replica_groups=mesh['dp'=8,'mp'=4] {'dp'}, dimensions={0} | all-to-all | bytes 655360 | tf_op jit(solution)/shard_map/all_to_all | solution.py:288
  108.2 0.8 fusion
  109.0 1.0 reshape.66
  110.0 4.4 %all-to-all-start.3 = ((bf16[4,36,2560]{2,1,0:T(8,128)(2,1)}), bf16[4,36,2560]{2,1,0:T(8,128)(2,1)}, u32[]{:S(2)}, u32[]{:S(2)}) async-start(bf16[4,36,2560]{2,1,0:T(8,128)(2,1)} %reshape.66), calls=%async_computation.3 | async-start | bytes 1638400 | tf_op jit(solution)/shard_map/all_to_all | solution.py:297
  114.5 0.2 broadcast_multiply_fusion
  114.7 1.2 mul.27.conv_ref
  116.0 19.4 %all-to-all-done.3 = bf16[4,36,2560]{2,1,0:T(8,128)(2,1)} async-done(((bf16[4,36,2560]{2,1,0:T(8,128)(2,1)}), bf16[4,36,2560]{2,1,0:T(8,128)(2,1)}, u32[]{:S(2)}, u32[]{:S(2)}) %all-to-all-start.3) | async-done | bytes 737312 | tf_op jit(solution)/shard_map/all_to_all | solution.py:297
  135.3 3.9 %copy.26 = bf16[4,36,2560]{1,2,0:T(8,128)(2,1)} copy(bf16[4,36,2560]{2,1,0:T(8,128)(2,1)} %all-to-all-done.3) | data formatting | bytes 1474560 | tf_op jit(solution)/shard_map/all_to_all | solution.py:297
  139.2 8.2 %copy.27 = bf16[20,4,8,36,16]{4,3,2,1,0:T(8,128)(2,1)} copy(bf16[20,4,8,36,16]{3,4,2,0,1:T(8,128)(2,1)} %bitcast.30) | data formatting | bytes 1474560 | tf_op jit(solution)/shard_map/transpose | solution.py:301
  147.4 7.2 %reshape.68.mixed_ref = bf16[640,576]{1,0:T(8,128)(2,1)S(1)} reshape(bf16[20,4,8,36,16]{4,3,2,1,0:T(8,128)(2,1)} %copy.27) | data formatting | bytes 1474560 | tf_op jit(solution)/shard_map/reshape | solution.py:301
  154.6 103.6 %slope_and_back.1 = bf16[640,576]{1,0:T(8,128)(2,1)S(1)} custom-call(f32[20]{0:T(128)S(1)} %copy-done.4, bf16[32,20,128,128]{3,2,1,0:T(8,128)(2,1)} %bitcast.25, bf16[32,20,128,128]{3,2,1,0:T(8,128)(2,1)} %bitcast.28, bf16[640,576]{1,0:T(8,128)(2,1)S(1)} %reshape.68.mixed_ref, bf16[320,320]{1,0:T(8,128)(2,1)S(1)} %mul.27.conv_ref, ...), custom_call_target="tpu_custom_call" | custom-call | tf_op jit(solution)/shard_map/slope_and_back/pallas_call | solution.py:304
  258.2 5.8 %reshape.69 = bf16[20,4,8,36,16]{4,3,2,1,0:T(8,128)(2,1)} reshape(bf16[640,576]{1,0:T(8,128)(2,1)S(1)} %slope_and_back.1) | data formatting | bytes 1474560 | tf_op jit(solution)/shard_map/reshape | solution.py:250
  264.0 7.6 %copy.29 = bf16[4,36,20,8,16]{1,4,3,2,0:T(8,128)(2,1)S(1)} copy(bf16[4,36,20,8,16]{4,1,3,0,2:T(8,128)(2,1)} %bitcast.27) | data formatting | bytes 1474560 | tf_op jit(solution)/shard_map/transpose | solution.py:251
  271.6 2.6 copy.30
  274.2 23.8 %all_to_all.32 = bf16[4,36,2560]{2,1,0:T(8,128)(2,1)S(1)} all-to-all(bf16[4,36,2560]{2,1,0:T(8,128)(2,1)} %copy.30), channel_id=1, replica_groups=mesh['dp'=8,'mp'=4] {'mp'}, dimensions={0} | all-to-all | bytes 1474560 | tf_op jit(solution)/shard_map/all_to_all | solution.py:252
  298.0 0.1 reshape.71
  298.1 0.4 convolution_bitcast_fusion
  298.6 13.5 %all_to_all.33 = f32[8,8,2560]{2,1,0:T(8,128)S(1)} all-to-all(f32[8,8,2560]{2,1,0:T(8,128)S(1)} %convolution_bitcast_fusion), channel_id=1, replica_groups=mesh['dp'=8,'mp'=4] {'dp'}, dimensions={0} | all-to-all | bytes 1310720 | tf_op jit(solution)/shard_map/all_to_all | solution.py:258
  312.2 2.3 weight_gradient.1
  314.6 2.4 copy.31
  (20 shorter events, 0.5 us)
Async XLA Ops:
  0.0 0.8 copy-start
  47.7 30.0 %copy-start.6 = (f32[64,144]{1,0:T(8,128)S(1)}, f32[64,144]{1,0:T(8,128)}, u32[]{:S(2)}) copy-start(f32[64,144]{1,0:T(8,128)} %constant.10.clone) | copy-start | bytes 110596
  50.3 32.6 %copy-start.5 = (bf16[4,2,20,20,128]{4,1,3,2,0:T(2,128)(2,1)S(1)}, bf16[4,2,20,20,128]{4,1,3,2,0:T(2,128)(2,1)}, u32[]{:S(2)}) copy-start(bf16[4,2,20,20,128]{4,1,3,2,0:T(2,128)(2,1)} %param.12) | copy-start | bytes 2457604
  79.0 15.1 %copy-start.3 = (f32[1,128]{1,0:T(1,128)S(1)}, f32[1,128]{1,0:T(1,128)}, u32[]{:S(2)}) copy-start(f32[1,128]{1,0:T(1,128)} %constant.14.clone.scale_ref) | copy-start | bytes 1540
  79.0 15.0 %all-to-all-start.1 = ((f32[8,8,2560]{2,1,0:T(8,128)}), f32[8,8,2560]{2,1,0:T(8,128)S(1)}, u32[]{:S(2)}, u32[]{:S(2)}) async-start(f32[8,8,2560]{2,1,0:T(8,128)} %convolution_bitcast_fusion.1), calls=%async_computation.1 | async-start | bytes 1310720 | tf_op jit(solution)/shard_map/all_to_all | solution.py:258
  98.2 16.2 %copy-start.7 = (bf16[20,20]{1,0:T(8,128)(2,1)S(1)}, bf16[20,20]{1,0:T(8,128)(2,1)}, u32[]{:S(2)}) copy-start(bf16[20,20]{1,0:T(8,128)(2,1)} %param.13) | copy-start | bytes 2404
  110.0 25.3 %all-to-all-start.3 = ((bf16[4,36,2560]{2,1,0:T(8,128)(2,1)}), bf16[4,36,2560]{2,1,0:T(8,128)(2,1)}, u32[]{:S(2)}, u32[]{:S(2)}) async-start(bf16[4,36,2560]{2,1,0:T(8,128)(2,1)} %reshape.66), calls=%async_computation.3 | async-start | bytes 1638400 | tf_op jit(solution)/shard_map/all_to_all | solution.py:297
  147.4 7.2 %copy-start.1 = (bf16[128,128]{1,0:T(8,128)(2,1)S(1)}, bf16[128,128]{1,0:T(8,128)(2,1)}, u32[]{:S(2)}) copy-start(bf16[128,128]{1,0:T(8,128)(2,1)} %constant.12.clone.table_y_ref) | copy-start | bytes 98308
  147.4 7.2 %copy-start.2 = (bf16[128,64]{1,0:T(8,128)(2,1)S(1)}, bf16[128,64]{1,0:T(8,128)(2,1)}, u32[]{:S(2)}) copy-start(bf16[128,64]{1,0:T(8,128)(2,1)} %constant.13.clone.inverse_y_ref) | copy-start | bytes 49156
  147.4 7.2 %copy-start.4 = (f32[20]{0:T(128)S(1)}, f32[20]{0:T(128)}, u32[]{:S(2)}) copy-start(f32[20]{0:T(128)} %bias_ref.1) | copy-start | bytes 244

commit v2 on v1

v2 whole, which is shorter than its diff:
```python
import functools
import math

import jax
import jax.numpy as jnp
import ml_dtypes
import numpy as np
from jax import lax
from jax.experimental import pallas as pl
from jax.experimental.pallas import tpu as pltpu
from jax.sharding import PartitionSpec as P

KX = 32
KY = 32
KZ = 16
ROWS = 16
VMEM_BYTES = 50 * 2**20

f32 = jnp.float32
bf16 = jnp.bfloat16


def kept_modes(count, length):
    indices = np.arange(count)
    return np.where(indices < count // 2, indices, length - count + indices)


def rounded(values):
    return np.asarray(values, np.float32).astype(ml_dtypes.bfloat16)


def split_parts(values):
    upper = rounded(values)
    return upper, rounded(values - upper.astype(np.float64))


def make_tables(x_cells, y_cells, z_cells, slabs):
    slab_len = x_cells // slabs
    kx = kept_modes(KX, x_cells)
    kx = np.where(kx >= x_cells // 2, kx - x_cells, kx)
    part = np.exp(-2j * math.pi * np.outer(kx, np.arange(slab_len)) / x_cells)
    left, scale, right = np.linalg.svd(part, full_matrices=False)
    rank = int(np.sum(scale > scale[0] * np.finfo(np.float32).eps))
    rank = min(rank + rank % 2, slab_len)
    left = left[:, :rank] * scale[:rank]
    right = right[:rank]
    shifts = np.exp(-2j * math.pi * np.outer(kx, np.arange(slabs) * slab_len) / x_cells)
    outer = shifts[:, :, None] * left[:, None, :]
    table_x = np.zeros((KX, 2, slabs, rank, 2))
    table_x[:, 0, :, :, 0] = outer.real
    table_x[:, 0, :, :, 1] = -outer.imag
    table_x[:, 1, :, :, 0] = outer.imag
    table_x[:, 1, :, :, 1] = outer.real
    table_x = table_x.reshape(KX * 2, slabs, rank * 2)
    table_x = np.stack([np.kron(table_x[:, m].T, np.eye(KZ)) for m in range(slabs)])
    wave_z = np.exp(-2j * math.pi * np.outer(np.arange(z_cells), np.arange(KZ)) / z_cells)
    inner = right.T[:, None, :, None] * wave_z[None, :, None, :]
    table_zx = np.zeros((slab_len, 2, z_cells, rank, 2, KZ))
    table_zx[:, 0, :, :, 0] = inner.real
    table_zx[:, 1, :, :, 0] = -inner.imag
    table_zx[:, 0, :, :, 1] = inner.imag
    table_zx[:, 1, :, :, 1] = inner.real
    table_zx = table_zx.reshape(slab_len, 2 * z_cells, rank * 2 * KZ)
    phase_y = 2.0 * math.pi * np.outer(kept_modes(KY, y_cells), np.arange(y_cells)) / y_cells
    table_y = np.concatenate([np.cos(phase_y), -np.sin(phase_y)], axis=0)
    return rank, table_x, table_zx, table_y


def dot(left, right, contract=((1,), (0,))):
    return lax.dot_general(left, right, (contract, ((), ())), preferred_element_type=f32)


def y_modes(pair, table, modes_ref, channel, z_cells, offset=0):
    both = dot(table, pair)
    half = 2 * KY
    total = both[:half] + both[half:]
    for i in range(2):
        one = total[:, i * z_cells : (i + 1) * z_cells].astype(bf16)
        rows = pl.ds((channel + i) * KY, KY)
        modes_ref[rows, offset : offset + z_cells] = one[:KY]
        modes_ref[rows, offset + z_cells : offset + 2 * z_cells] = one[KY:]


def column_chunks(lanes):
    return [(start, min(start + 256, lanes)) for start in range(0, lanes, 256)]


def store_blocks(total_ref, out_ref, channels):
    blocks, rows, _ = out_ref.shape
    ky_local = rows // channels
    group = max(1, ROWS // ky_local)
    for b in range(blocks):
        for c in range(0, channels, group):
            parts = [
                total_ref[(c + i) * KY + b * ky_local : (c + i) * KY + (b + 1) * ky_local, :]
                for i in range(group)
            ]
            out_ref[b, c * ky_local : (c + group) * ky_local, :] = jnp.concatenate(
                parts, axis=0
            ).astype(bf16)


def forward_kernel(fields_ref, table_y_ref, table_zx_ref, out_ref, first_ref, second_ref, total_ref):
    cells, channels, _, z_cells = fields_ref.shape
    lanes = total_ref.shape[1]
    step = pl.program_id(0)
    table = table_y_ref[...]

    @pl.when(step == 0)
    def _():
        total_ref[...] = jnp.zeros_like(total_ref)

    def inner(modes_ref, cell, start, stop):
        both = table_zx_ref[cell : cell + 2, :, start:stop].reshape(4 * z_cells, stop - start)
        total_ref[:, start:stop] += dot(modes_ref[...], both)

    pending = []
    for half, modes_ref in enumerate((first_ref, second_ref)):
        cell = 2 * half
        for c in range(0, channels, 2):
            for i in range(2):
                pair = jnp.concatenate(
                    [fields_ref[cell + i, c], fields_ref[cell + i, c + 1]], axis=1
                )
                y_modes(pair, table, modes_ref, c, z_cells, 2 * i * z_cells)
            if pending and c % 4 == 2:
                pending.pop(0)()
        for todo in pending:
            todo()
        pending = [
            functools.partial(inner, modes_ref, cell, start, stop)
            for start, stop in column_chunks(lanes)
        ]
    for todo in pending:
        todo()

    @pl.when(step == pl.num_programs(0) - 1)
    def _():
        store_blocks(total_ref, out_ref, channels)


def gelu_slope(values):
    size = jnp.abs(values)
    bell = jnp.exp2(values * values * (-0.5 * math.log2(math.e)))
    t = pl.reciprocal(1.0 + size * (0.3275911 * math.sqrt(0.5)), approx=True)
    tail = t * (
        0.5 * 0.254829592
        + t * (0.5 * -0.284496736 + t * (0.5 * 1.421413741 + t * (0.5 * -1.453152027 + t * (0.5 * 1.061405429))))
    )
    part = bell * (size * 0.3989422804014327 - tail)
    return jnp.where(values >= 0.0, 1.0 + part, -part)


def slope_kernel(
    bias_ref,
    fields_first_ref,
    fields_odd_ref,
    fields_next_ref,
    cotangent_ref,
    mixed_ref,
    conv_ref,
    table_y_ref,
    inverse_y_ref,
    zx_before_ref,
    zx_even_ref,
    zx_odd_ref,
    zx_next_ref,
    out_ref,
    rows_ref,
    back_even_ref,
    back_odd_ref,
    pre_even_ref,
    pre_odd_ref,
    modes_even_ref,
    modes_odd_ref,
    total_ref,
):
    _, channels, y_cells, z_cells = cotangent_ref.shape
    lanes = total_ref.shape[1]
    count = channels * KY
    step = pl.program_id(0)
    last = pl.num_programs(0) - 1
    table = table_y_ref[...]
    inverse_y = inverse_y_ref[...]
    mixing = conv_ref[...]

    def ahead(fields_ref, zx_ref, back_ref, pre_ref):
        def inverse(start, stop):
            back_ref[start:stop, :] = dot(
                rows_ref[start:stop, :], zx_ref[0], ((1,), (1,))
            ).astype(bf16)

        def convolve(g):
            pair = jnp.concatenate(
                [
                    fields_ref[0, :, g : g + ROWS, :].reshape(channels * ROWS, z_cells),
                    fields_ref[0, :, g + ROWS : g + 2 * ROWS, :].reshape(channels * ROWS, z_cells),
                ],
                axis=1,
            )
            conv = dot(mixing, pair)
            for i in range(2):
                rows = slice(g + i * ROWS, g + (i + 1) * ROWS)
                pre_ref[:, rows, :] = conv[:, i * z_cells : (i + 1) * z_cells].reshape(
                    channels, ROWS, z_cells
                )

        return [
            functools.partial(inverse, 0, count // 2),
            functools.partial(inverse, count // 2, count),
        ] + [functools.partial(convolve, g) for g in range(0, y_cells, 2 * ROWS)]

    def behind(modes_ref, zx_ref):
        def inner(start, stop):
            total_ref[:, start:stop] += dot(modes_ref[...], zx_ref[0, :, start:stop])

        return [functools.partial(inner, start, stop) for start, stop in column_chunks(lanes)]

    def here(cell, back_ref, pre_ref, modes_ref, o):
        columns = []
        for i in range(2):
            one = back_ref[(o + i) * KY : (o + i + 1) * KY, :]
            columns.append(jnp.concatenate([one[:, :z_cells], one[:, z_cells:]], axis=0))
        spectral = dot(inverse_y, jnp.concatenate(columns, axis=1))
        deltas = []
        for i in range(2):
            pre = spectral[:, i * z_cells : (i + 1) * z_cells] + pre_ref[o + i] + bias_ref[o + i]
            deltas.append((cotangent_ref[cell, o + i].astype(f32) * gelu_slope(pre)).astype(bf16))
        y_modes(jnp.concatenate(deltas, axis=1), table, modes_ref, o, z_cells)

    @pl.when(step == 0)
    def _():
        blocks = mixed_ref.shape[0]
        per_block = mixed_ref.shape[1]
        ky_local = per_block // channels
        for b in range(blocks):
            total_ref[b * per_block : (b + 1) * per_block, :] = mixed_ref[b].astype(f32)
        for o in range(channels):
            parts = [
                total_ref[b * per_block + o * ky_local : b * per_block + (o + 1) * ky_local, :]
                for b in range(blocks)
            ]
            rows_ref[o * KY : (o + 1) * KY, :] = jnp.concatenate(parts, axis=0).astype(bf16)
        total_ref[...] = jnp.zeros_like(total_ref)
        modes_odd_ref[...] = jnp.zeros_like(modes_odd_ref)
        for todo in ahead(fields_first_ref, zx_even_ref, back_even_ref, pre_even_ref):
            todo()

    even = (back_even_ref, pre_even_ref, modes_even_ref)
    odd = (back_odd_ref, pre_odd_ref, modes_odd_ref)
    for cell, own, beside in (
        (
            0,
            even,
            behind(modes_odd_ref, zx_before_ref)
            + ahead(fields_odd_ref, zx_odd_ref, back_odd_ref, pre_odd_ref),
        ),
        (
            1,
            odd,
            behind(modes_even_ref, zx_even_ref)
            + ahead(fields_next_ref, zx_next_ref, back_even_ref, pre_even_ref),
        ),
    ):
        for o in range(0, channels, 2):
            if beside:
                beside.pop(0)()
            here(cell, *own, o)
        for todo in beside:
            todo()

    @pl.when(step == last)
    def _():
        for todo in behind(modes_odd_ref, zx_odd_ref):
            todo()
        store_blocks(total_ref, out_ref, channels)


def to_modes_kernel(coefs_ref, upper_ref, lower_ref, out_ref):
    total = jnp.zeros((coefs_ref.shape[1], upper_ref.shape[2]), f32)
    for m in range(coefs_ref.shape[0]):
        total += dot(coefs_ref[m], upper_ref[m]) + dot(coefs_ref[m], lower_ref[m])
    width = out_ref.shape[2]
    for i in range(out_ref.shape[0]):
        out_ref[i] = total[:, i * width : (i + 1) * width]


def from_modes_kernel(modes_ref, upper_ref, lower_ref, out_ref):
    modes = jnp.concatenate([modes_ref[i] for i in range(modes_ref.shape[0])], axis=1)
    flip = ((1,), (1,))
    out_ref[0] = (dot(modes, upper_ref[0], flip) + dot(modes, lower_ref[0], flip)).astype(bf16)


def swap_groups(parts):
    lanes = parts[0].shape[1]
    group = lax.broadcasted_iota(jnp.int32, parts[0].shape, 1) // KZ
    results = []
    for j in range(len(parts)):
        total = parts[j]
        for i, part in enumerate(parts):
            if i != j:
                moved = pltpu.roll(part, ((i - j) * KZ) % lanes, 1)
                total = jnp.where(group == i, moved, total)
        results.append(total)
    return results


def open_rows(wire_ref, s, channels):
    ky_local = wire_ref.shape[1] // channels
    return swap_groups(
        [wire_ref[s, pl.ds(k, channels, stride=ky_local), :] for k in range(ky_local)]
    )


def mix_kernel(blocked, spectra_ref, weight_ref, scale_ref, out_ref, opened_ref, rows_ref):
    samples = spectra_ref.shape[0]
    kx_local, _, channels, _, mode_cells = weight_ref.shape
    scale = scale_ref[...]

    def one_sample(s, carry):
        if blocked:
            for g, part in enumerate(open_rows(spectra_ref, s, channels)):
                opened_ref[s, g] = part
        else:
            opened_ref[s] = spectra_ref[s]
        results = []
        for k in range(kx_local):
            real = jnp.zeros((channels, mode_cells), f32)
            imag = jnp.zeros((channels, mode_cells), f32)
            for c in range(channels):
                spec_re = opened_ref[s, 2 * k, c : c + 1, :]
                spec_im = opened_ref[s, 2 * k + 1, c : c + 1, :]
                real_w = weight_ref[k, 0, c].astype(f32)
                imag_w = weight_ref[k, 1, c].astype(f32)
                real += spec_re * real_w - spec_im * imag_w
                imag += spec_re * imag_w + spec_im * real_w
            results += [real * scale, imag * scale]
        if blocked:
            ky_local = rows_ref.shape[0] // channels
            for k, part in enumerate(swap_groups(results)):
                rows_ref[pl.ds(k, channels, stride=ky_local), :] = part
            out_ref[s] = rows_ref[...].astype(bf16)
        else:
            for g, part in enumerate(results):
                out_ref[s, g] = part.astype(bf16)
        return carry

    lax.fori_loop(0, samples, one_sample, 0)


def grad_kernel(blocked, spectra_ref, back_ref, scale_ref, out_ref, opened_ref):
    kx_local, _, channels, _, mode_cells = out_ref.shape
    samples = spectra_ref.shape[0]
    scale = scale_ref[...]
    for s in range(samples):
        if blocked:
            for g, part in enumerate(open_rows(back_ref, s, channels)):
                opened_ref[s, g] = part * scale
        else:
            opened_ref[s] = back_ref[s] * scale

    def one_channel(c, carry):
        for k in range(kx_local):
            real = jnp.zeros((channels, mode_cells), f32)
            imag = jnp.zeros((channels, mode_cells), f32)
            for s in range(samples):
                spec_re = spectra_ref[s, 2 * k, pl.ds(c, 1), :]
                spec_im = spectra_ref[s, 2 * k + 1, pl.ds(c, 1), :]
                back_re = opened_ref[s, 2 * k]
                back_im = opened_ref[s, 2 * k + 1]
                real += spec_re * back_re + spec_im * back_im
                imag += spec_re * back_im - spec_im * back_re
            out_ref[k, 0, c] = real
            out_ref[k, 1, c] = imag
        return carry

    lax.fori_loop(0, channels, one_channel, 0)


def shards(fields, cotangent, spectral_weight, conv_weight, conv_bias):
    _, slab_len, channels, y_cells, z_cells = fields.shape
    slabs = lax.axis_size("mp")
    data_count = lax.axis_size("dp")
    kx_local = spectral_weight.shape[0]
    ky_local = KY // slabs
    x_cells = slab_len * slabs
    rank, table_x, table_zx, table_y = make_tables(x_cells, y_cells, z_cells, slabs)
    lanes = rank * 2 * KZ
    x_upper, x_lower = (jnp.asarray(part) for part in split_parts(table_x))
    table_zx = jnp.asarray(rounded(table_zx))
    y_parts = jnp.asarray(np.concatenate(split_parts(table_y), axis=0))
    inverse_y = jnp.asarray(rounded(table_y.T))
    weight_z = np.where(np.arange(KZ) == 0, 1.0, 2.0) / (x_cells * y_cells * z_cells)
    scale = jnp.asarray(np.tile(weight_z, ky_local)[None].astype(np.float32))
    mixing = jnp.kron(conv_weight.T, jnp.eye(ROWS, dtype=bf16))
    mode_cells = ky_local * KZ
    groups = 2 * kx_local
    rows = channels * ky_local
    width = groups * KZ
    blocked = groups == ky_local and width % 128 == 0

    def whole(shape):
        return pl.BlockSpec(shape, lambda *x: (0,) * len(shape))

    def cells_at(index, count=1):
        return pl.BlockSpec((count, channels, y_cells, z_cells), lambda x: (index(x), 0, 0, 0))

    def zx_at(index, count=1):
        return pl.BlockSpec((count, 2 * z_cells, lanes), lambda x: (index(x), 0, 0))

    params = pltpu.CompilerParams(
        dimension_semantics=("arbitrary",), vmem_limit_bytes=VMEM_BYTES
    )
    loose = pltpu.CompilerParams(vmem_limit_bytes=VMEM_BYTES)
    coefs_shape = (slabs, rows, lanes)
    coefs_out = jax.ShapeDtypeStruct(coefs_shape, bf16)
    total_shape = (channels * KY, lanes)
    modes_shape = (channels * KY, 2 * z_cells)

    def over(values, axis):
        return lax.all_to_all(values, axis, split_axis=0, concat_axis=0, tiled=True)

    def across_samples(coefs):
        per_step = max(1, 256 // width)
        block = pl.BlockSpec((slabs, lanes, per_step * width), lambda d: (0, 0, d))
        modes = pl.pallas_call(
            to_modes_kernel,
            grid=(data_count // per_step,),
            in_specs=[whole(coefs_shape), block, block],
            out_specs=pl.BlockSpec((per_step, rows, width), lambda d: (d, 0, 0)),
            out_shape=jax.ShapeDtypeStruct((data_count, rows, width), f32),
            compiler_params=params,
        )(over(coefs, "mp"), x_upper, x_lower)
        moved = over(modes, "dp")
        if not blocked:
            moved = moved.reshape(data_count, channels, ky_local, groups, KZ)
            moved = jnp.transpose(moved, (0, 3, 1, 2, 4))
            moved = moved.reshape(data_count, groups, channels, mode_cells)
        return moved

    with jax.named_scope("forward_fields"):
        coefs = pl.pallas_call(
            forward_kernel,
            grid=(slab_len // 4,),
            in_specs=[cells_at(lambda x: x, 4), whole(y_parts.shape), zx_at(lambda x: x, 4)],
            out_specs=whole(coefs_shape),
            out_shape=coefs_out,
            scratch_shapes=[
                pltpu.VMEM((channels * KY, 4 * z_cells), bf16),
                pltpu.VMEM((channels * KY, 4 * z_cells), bf16),
                pltpu.VMEM(total_shape, f32),
            ],
            compiler_params=params,
        )(fields[0], y_parts, table_zx)
    spectra = across_samples(coefs)

    opened_shape = (data_count, groups, channels, mode_cells)
    mixed_shape = (data_count, rows, width) if blocked else opened_shape
    with jax.named_scope("mix_modes"):
        local_mixed, opened = pl.pallas_call(
            functools.partial(mix_kernel, blocked),
            out_shape=[
                jax.ShapeDtypeStruct(mixed_shape, bf16),
                jax.ShapeDtypeStruct(opened_shape, f32),
            ],
            scratch_shapes=[pltpu.VMEM((rows, width), f32)],
            compiler_params=loose,
        )(spectra, spectral_weight, scale)
    if not blocked:
        local_mixed = local_mixed.reshape(data_count, groups, channels, ky_local, KZ)
        local_mixed = jnp.transpose(local_mixed, (0, 2, 3, 1, 4)).reshape(data_count, rows, width)
    slab_block = pl.BlockSpec((1, lanes, KX * 2 * KZ), lambda m: (m, 0, 0))
    slab_mixed = pl.pallas_call(
        from_modes_kernel,
        grid=(slabs,),
        in_specs=[whole((data_count, rows, width)), slab_block, slab_block],
        out_specs=pl.BlockSpec((1, rows, lanes), lambda m: (m, 0, 0)),
        out_shape=coefs_out,
        compiler_params=params,
    )(over(local_mixed, "dp"), x_upper, x_lower)
    mixed_coefs = over(slab_mixed, "mp")

    with jax.named_scope("slope_and_back"):
        back_coefs = pl.pallas_call(
            slope_kernel,
            grid=(slab_len // 2,),
            in_specs=[
                pl.BlockSpec(memory_space=pltpu.SMEM),
                cells_at(lambda x: 0),
                cells_at(lambda x: 2 * x + 1),
                cells_at(lambda x: jnp.minimum(2 * x + 2, slab_len - 1)),
                cells_at(lambda x: x, 2),
                whole(coefs_shape),
                whole(mixing.shape),
                whole(y_parts.shape),
                whole(inverse_y.shape),
                zx_at(lambda x: jnp.maximum(2 * x - 1, 0)),
                zx_at(lambda x: 2 * x),
                zx_at(lambda x: 2 * x + 1),
                zx_at(lambda x: jnp.minimum(2 * x + 2, slab_len - 1)),
            ],
            out_specs=whole(coefs_shape),
            out_shape=coefs_out,
            scratch_shapes=[pltpu.VMEM(total_shape, bf16)]
            + [pltpu.VMEM(modes_shape, bf16)] * 2
            + [pltpu.VMEM((channels, y_cells, z_cells), f32)] * 2
            + [pltpu.VMEM(modes_shape, bf16)] * 2
            + [pltpu.VMEM(total_shape, f32)],
            compiler_params=params,
        )(
            conv_bias,
            fields[0],
            fields[0],
            fields[0],
            cotangent[0],
            mixed_coefs,
            mixing,
            y_parts,
            inverse_y,
            table_zx,
            table_zx,
            table_zx,
            table_zx,
        )
    back = across_samples(back_coefs)

    with jax.named_scope("weight_gradient"):
        return pl.pallas_call(
            functools.partial(grad_kernel, blocked),
            out_shape=jax.ShapeDtypeStruct(spectral_weight.shape, f32),
            scratch_shapes=[pltpu.VMEM(opened_shape, f32)],
            compiler_params=loose,
        )(opened, back, scale)


def solution(mesh):
    return jax.shard_map(
        shards,
        mesh=mesh,
        in_specs=(
            P("dp", "mp", None, None, None),
            P("dp", "mp", None, None, None),
            P("dp", None, None, None, "mp"),
            P(),
            P(),
        ),
        out_specs=P("dp", None, None, None, "mp"),
        check_vma=False,
    )
```

time: 319 us -> 258 us (0.81)
  local copies, waits for them, and re-layouts: 57.5 us -> 6.28 us
    reshape x11 -> x0, local copies, waits for them, and re-layouts: 25.6 us -> none  [the longest x2 11.5 us: to_modes(): packed = coefs.reshape(channels, slabs, ky_local, rank * 2, KZ)]
    transpose x3 -> x0, local copies, waits for them, and re-layouts: 23.4 us -> none  [the longest x2 15.2 us: to_modes(): packed = jnp.transpose(packed, (1, 3, 0, 2, 4)).reshape(slabs, rank * 2, -1)]
    all_to_all x1 -> x0, local copies, waits for them, and re-layouts: 3.85 us -> none  [shards(): lax.all_to_all(slab_mixed.reshape(slabs, rank * 2, -1), 'mp', split_axis=...]
    pallas_call x4 -> x7, Pallas kernels: 143 us -> 141 us  [the longest x1 93.4 us: shards(): pl.pallas_call(slope_kernel, grid=(slab_len // 2,), in_specs=[pl.BlockSpe...]
  transfers between devices with their start and end apart: 2 -> 2, of which waited for: 2 -> 2; matrix products, arithmetic and copies ran while one was open for 1% -> 2% of each run, Pallas kernels for 0% -> 0%
where the time goes in v2:
time: 258 us; the launch traced here: 257 us
  Pallas kernels  141 us (55%)
  blocking collectives  73.4 us (28%)
  waiting for transfers between devices  27.5 us (11%)
  starting transfers between devices  7.35 us (3%)
  local copies, waits for them, and re-layouts  6.28 us (2%)
    pallas_call x1, Pallas kernels, shards(): pl.pallas_call(slope_kernel, grid=(slab_len // 2,), in_specs=[pl.BlockSpe...  93.4 us
    all_to_all x4, blocking collectives, over(): return lax.all_to_all(values, axis, split_axis=0, concat_axis=0, tiled=True)  73.4 us
    all_to_all x2, waiting for transfers between devices, over(): return lax.all_to_all(values, axis, split_axis=0, concat_axis=0, tiled=True)  27.5 us
    pallas_call x1, Pallas kernels, shards(): pl.pallas_call(forward_kernel, grid=(slab_len // 4,), in_specs=[cells_at(...  18.1 us
    pallas_call x2, Pallas kernels, across_samples(): pl.pallas_call(to_modes_kernel, grid=(data_count // per_step,), in_specs=...  11.9 us
    all_to_all x2, starting transfers between devices, over(): return lax.all_to_all(values, axis, split_axis=0, concat_axis=0, tiled=True)  7.35 us
    pallas_call x1, Pallas kernels, shards(): pl.pallas_call(from_modes_kernel, grid=(slabs,), in_specs=[whole((data_co...  6.97 us
    pallas_call x1, Pallas kernels, shards(): pl.pallas_call(functools.partial(mix_kernel, blocked), out_shape=[jax.Sha...  6.5 us
  transfers between devices with their start and end apart: 2, of which 2 were waited for; matrix products, arithmetic and copies ran while one was open for 2% of the time, Pallas kernels for 0%

profile of v2, /device:TPU:0, one launch (start us, length us, event | category | flops | bytes accessed | tf_op | source)
XLA Modules:
  0.0 257.1 jit_solution(13852679258338606095)
XLA Ops:
  0.0 0.0 copy-start
  0.0 0.8 copy-done
  0.8 18.1 %forward_fields.1 = bf16[4,160,576]{2,1,0:T(8,128)(2,1)S(1)} custom-call(bf16[32,20,128,128]{3,2,1,0:T(8,128)(2,1)} %bitcast.3, bf16[128,128]{1,0:T(8,128)(2,1)S(1)} %copy-done, bf16[32,256,576]{2,1,0:T(8,128)(2,1)} %constant.14.clone.table_zx_ref.zx_before_ref.zx_even_ref.zx_odd_ref.zx_next_ref), custom_call_target="tpu_custom_call" | custom-call | tf_op jit(solution)/shard_map/forward_fields/pallas_call | solution.py:442
  18.9 26.9 %all_to_all.30.coefs_ref = bf16[4,160,576]{2,1,0:T(8,128)(2,1)S(1)} all-to-all(bf16[4,160,576]{2,1,0:T(8,128)(2,1)S(1)} %forward_fields.1), channel_id=1, replica_groups=mesh['dp'=8,'mp'=4] {'mp'}, dimensions={0} | all-to-all | bytes 1474560 | tf_op jit(solution)/shard_map/all_to_all | solution.py:421
  45.8 0.0 copy-start.5
  45.8 6.4 %shard_map.109 = f32[8,160,128]{2,1,0:T(8,128)} custom-call(bf16[4,160,576]{2,1,0:T(8,128)(2,1)S(1)} %all_to_all.30.coefs_ref, bf16[4,576,1024]{2,1,0:T(8,128)(2,1)} %constant.12.clone.upper_ref, bf16[4,576,1024]{2,1,0:T(8,128)(2,1)} %constant.13.clone.lower_ref), custom_call_target="tpu_custom_call" | custom-call | tf_op jit(solution)/shard_map/pallas_call | solution.py:426
  52.2 0.0 copy-start.3
  52.2 3.9 %all-to-all-start.1 = ((f32[8,160,128]{2,1,0:T(8,128)}), f32[8,160,128]{2,1,0:T(8,128)S(1)}, u32[]{:S(2)}, u32[]{:S(2)}) async-start(f32[8,160,128]{2,1,0:T(8,128)} %shard_map.109), calls=%async_computation.1 | async-start | bytes 1310720 | tf_op jit(solution)/shard_map/all_to_all | solution.py:421
  56.0 0.0 copy-done.5
  56.0 0.1 copy.15.weight_ref
  56.2 11.0 %all-to-all-done.1.spectra_ref = f32[8,160,128]{2,1,0:T(8,128)S(1)} async-done(((f32[8,160,128]{2,1,0:T(8,128)}), f32[8,160,128]{2,1,0:T(8,128)S(1)}, u32[]{:S(2)}, u32[]{:S(2)}) %all-to-all-start.1) | async-done | bytes 655392 | tf_op jit(solution)/shard_map/all_to_all | solution.py:421
  67.2 0.0 copy-done.3
  67.2 6.5 %mix_modes.1 = (bf16[8,160,128]{2,1,0:T(8,128)(2,1)S(1)}, f32[8,8,20,128]{3,2,1,0:T(8,128)S(1)}) custom-call(f32[8,160,128]{2,1,0:T(8,128)S(1)} %all-to-all-done.1.spectra_ref, bf16[4,2,20,20,128]{4,3,2,1,0:T(8,128)(2,1)S(1)} %copy.15.weight_ref, f32[1,128]{1,0:T(1,128)S(1)} %copy-done.3), custom_call_target="tpu_custom_call" | custom-call | tf_op jit(solution)/shard_map/mix_modes/pallas_call | solution.py:460
  73.7 10.0 %all_to_all.31.modes_ref = bf16[8,160,128]{2,1,0:T(8,128)(2,1)S(1)} all-to-all(bf16[8,160,128]{2,1,0:T(8,128)(2,1)S(1)} %get-tuple-element.8), channel_id=1, replica_groups=mesh['dp'=8,'mp'=4] {'dp'}, dimensions={0} | all-to-all | bytes 655360 | tf_op jit(solution)/shard_map/all_to_all | solution.py:421
  83.7 7.0 %shard_map.110 = bf16[4,160,576]{2,1,0:T(8,128)(2,1)} custom-call(bf16[8,160,128]{2,1,0:T(8,128)(2,1)S(1)} %all_to_all.31.modes_ref, bf16[4,576,1024]{2,1,0:T(8,128)(2,1)} %constant.12.clone.upper_ref, bf16[4,576,1024]{2,1,0:T(8,128)(2,1)} %constant.13.clone.lower_ref), custom_call_target="tpu_custom_call" | custom-call | tf_op jit(solution)/shard_map/pallas_call | solution.py:473
  90.7 3.5 %all-to-all-start.3 = ((bf16[4,160,576]{2,1,0:T(8,128)(2,1)}), bf16[4,160,576]{2,1,0:T(8,128)(2,1)S(1)}, u32[]{:S(2)}, u32[]{:S(2)}) async-start(bf16[4,160,576]{2,1,0:T(8,128)(2,1)} %shard_map.110), calls=%async_computation.3 | async-start | bytes 1638400 | tf_op jit(solution)/shard_map/all_to_all | solution.py:421
  94.2 0.0 copy-done.6
  94.2 0.1 copy.16
  94.3 0.0 copy-start.2
  94.3 0.0 copy-start.4
  94.3 1.5 broadcast_multiply_fusion
  95.8 2.8 %mul.27.conv_ref = bf16[320,320]{1,0:T(8,128)(2,1)S(1)} reshape(bf16[20,16,20,16]{3,2,1,0:T(8,128)(2,1)} %broadcast_multiply_fusion) | data formatting | bytes 409600 | tf_op jit(solution)/shard_map/jit(kron)/mul | solution.py:395
  98.7 16.5 %all-to-all-done.3.mixed_ref = bf16[4,160,576]{2,1,0:T(8,128)(2,1)S(1)} async-done(((bf16[4,160,576]{2,1,0:T(8,128)(2,1)}), bf16[4,160,576]{2,1,0:T(8,128)(2,1)S(1)}, u32[]{:S(2)}, u32[]{:S(2)}) %all-to-all-start.3) | async-done | bytes 737312 | tf_op jit(solution)/shard_map/all_to_all | solution.py:421
  115.2 0.0 copy-done.1
  115.2 0.0 copy-done.2
  115.2 0.0 copy-done.4
  115.2 93.4 %slope_and_back.1 = bf16[4,160,576]{2,1,0:T(8,128)(2,1)S(1)} custom-call(f32[20]{0:T(128)S(1)} %copy-done.4, bf16[32,20,128,128]{3,2,1,0:T(8,128)(2,1)} %bitcast.4, bf16[32,20,128,128]{3,2,1,0:T(8,128)(2,1)} %bitcast.5, bf16[32,20,128,128]{3,2,1,0:T(8,128)(2,1)} %bitcast.6, bf16[32,20,128,128]{3,2,1,0:T(8,128)(2,1)} %bitcast.7, ...), custom_call_target="tpu_custom_call" | custom-call | tf_op jit(solution)/shard_map/slope_and_back/pallas_call | solution.py:484
  208.6 22.8 %all_to_all.32.coefs_ref = bf16[4,160,576]{2,1,0:T(8,128)(2,1)S(1)} all-to-all(bf16[4,160,576]{2,1,0:T(8,128)(2,1)S(1)} %slope_and_back.1), channel_id=1, replica_groups=mesh['dp'=8,'mp'=4] {'mp'}, dimensions={0} | all-to-all | bytes 1474560 | tf_op jit(solution)/shard_map/all_to_all | solution.py:421
  231.4 5.6 %shard_map.111 = f32[8,160,128]{2,1,0:T(8,128)S(1)} custom-call(bf16[4,160,576]{2,1,0:T(8,128)(2,1)S(1)} %all_to_all.32.coefs_ref, bf16[4,576,1024]{2,1,0:T(8,128)(2,1)} %constant.12.clone.upper_ref, bf16[4,576,1024]{2,1,0:T(8,128)(2,1)} %constant.13.clone.lower_ref), custom_call_target="tpu_custom_call" | custom-call | tf_op jit(solution)/shard_map/pallas_call | solution.py:426
  236.9 13.7 %all_to_all.33.back_ref = f32[8,160,128]{2,1,0:T(8,128)S(1)} all-to-all(f32[8,160,128]{2,1,0:T(8,128)S(1)} %shard_map.111), channel_id=1, replica_groups=mesh['dp'=8,'mp'=4] {'dp'}, dimensions={0} | all-to-all | bytes 1310720 | tf_op jit(solution)/shard_map/all_to_all | solution.py:421
  250.7 4.0 %weight_gradient.1 = f32[4,2,20,20,128]{4,3,2,1,0:T(8,128)S(1)} custom-call(f32[8,8,20,128]{3,2,1,0:T(8,128)S(1)} %get-tuple-element.7.spectra_ref, f32[8,160,128]{2,1,0:T(8,128)S(1)} %all_to_all.33.back_ref, f32[1,128]{1,0:T(1,128)S(1)} %copy-done.3), custom_call_target="tpu_custom_call" | custom-call | tf_op jit(solution)/shard_map/weight_gradient/pallas_call | solution.py:528
  254.7 2.4 copy.17
  (3 shorter events, 0.0 us)
Async XLA Ops:
  0.0 0.8 copy-start
  45.8 10.2 %copy-start.5 = (bf16[4,2,20,20,128]{4,1,3,2,0:T(2,128)(2,1)S(1)}, bf16[4,2,20,20,128]{4,1,3,2,0:T(2,128)(2,1)}, u32[]{:S(2)}) copy-start(bf16[4,2,20,20,128]{4,1,3,2,0:T(2,128)(2,1)} %param.13) | copy-start | bytes 2457604
  52.2 15.0 %copy-start.3 = (f32[1,128]{1,0:T(1,128)S(1)}, f32[1,128]{1,0:T(1,128)}, u32[]{:S(2)}) copy-start(f32[1,128]{1,0:T(1,128)} %constant.17.clone.scale_ref) | copy-start | bytes 1540
  52.2 15.0 %all-to-all-start.1 = ((f32[8,160,128]{2,1,0:T(8,128)}), f32[8,160,128]{2,1,0:T(8,128)S(1)}, u32[]{:S(2)}, u32[]{:S(2)}) async-start(f32[8,160,128]{2,1,0:T(8,128)} %shard_map.109), calls=%async_computation.1 | async-start | bytes 1310720 | tf_op jit(solution)/shard_map/all_to_all | solution.py:421
  83.7 10.5 %copy-start.6 = (bf16[20,20]{1,0:T(8,128)(2,1)S(1)}, bf16[20,20]{1,0:T(8,128)(2,1)}, u32[]{:S(2)}) copy-start(bf16[20,20]{1,0:T(8,128)(2,1)} %param.14) | copy-start | bytes 2404
  90.7 24.5 %all-to-all-start.3 = ((bf16[4,160,576]{2,1,0:T(8,128)(2,1)}), bf16[4,160,576]{2,1,0:T(8,128)(2,1)S(1)}, u32[]{:S(2)}, u32[]{:S(2)}) async-start(bf16[4,160,576]{2,1,0:T(8,128)(2,1)} %shard_map.110), calls=%async_computation.3 | async-start | bytes 1638400 | tf_op jit(solution)/shard_map/all_to_all | solution.py:421
  94.3 20.9 %copy-start.1 = (bf16[128,128]{1,0:T(8,128)(2,1)S(1)}, bf16[128,128]{1,0:T(8,128)(2,1)}, u32[]{:S(2)}) copy-start(bf16[128,128]{1,0:T(8,128)(2,1)} %constant.15.clone.table_y_ref) | copy-start | bytes 98308
  94.3 20.9 %copy-start.2 = (bf16[128,64]{1,0:T(8,128)(2,1)S(1)}, bf16[128,64]{1,0:T(8,128)(2,1)}, u32[]{:S(2)}) copy-start(bf16[128,64]{1,0:T(8,128)(2,1)} %constant.16.clone.inverse_y_ref) | copy-start | bytes 49156
  94.3 20.8 %copy-start.4 = (f32[20]{0:T(128)S(1)}, f32[20]{0:T(128)}, u32[]{:S(2)}) copy-start(f32[20]{0:T(128)} %bias_ref.1) | copy-start | bytes 244

commit v3 on v2

--- a/solution.py
+++ b/solution.py
@@ -163,8 +163,10 @@
     inverse_y_ref,
     zx_before_ref,
     zx_even_ref,
-    zx_odd_ref,
-    zx_next_ref,
+    zx_last_ref,
+    inverse_first_ref,
+    inverse_odd_ref,
+    inverse_next_ref,
     out_ref,
     rows_ref,
     back_even_ref,
@@ -184,11 +186,9 @@
     inverse_y = inverse_y_ref[...]
     mixing = conv_ref[...]
 
-    def ahead(fields_ref, zx_ref, back_ref, pre_ref):
+    def ahead(fields_ref, inverse_ref, back_ref, pre_ref):
         def inverse(start, stop):
-            back_ref[start:stop, :] = dot(
-                rows_ref[start:stop, :], zx_ref[0], ((1,), (1,))
-            ).astype(bf16)
+            back_ref[start:stop, :] = dot(rows_ref[start:stop, :], inverse_ref[0]).astype(bf16)
 
         def convolve(g):
             pair = jnp.concatenate(
@@ -216,17 +216,19 @@
 
         return [functools.partial(inner, start, stop) for start, stop in column_chunks(lanes)]
 
-    def here(cell, back_ref, pre_ref, modes_ref, o):
+    def inverse_pair(back_ref, o):
         columns = []
         for i in range(2):
             one = back_ref[(o + i) * KY : (o + i + 1) * KY, :]
             columns.append(jnp.concatenate([one[:, :z_cells], one[:, z_cells:]], axis=0))
-        spectral = dot(inverse_y, jnp.concatenate(columns, axis=1))
+        return dot(inverse_y, jnp.concatenate(columns, axis=1))
+
+    def slope_pair(cell, spectral, pre_ref, o):
         deltas = []
         for i in range(2):
             pre = spectral[:, i * z_cells : (i + 1) * z_cells] + pre_ref[o + i] + bias_ref[o + i]
             deltas.append((cotangent_ref[cell, o + i].astype(f32) * gelu_slope(pre)).astype(bf16))
-        y_modes(jnp.concatenate(deltas, axis=1), table, modes_ref, o, z_cells)
+        return jnp.concatenate(deltas, axis=1)
 
     @pl.when(step == 0)
     def _():
@@ -243,35 +245,40 @@
             rows_ref[o * KY : (o + 1) * KY, :] = jnp.concatenate(parts, axis=0).astype(bf16)
         total_ref[...] = jnp.zeros_like(total_ref)
         modes_odd_ref[...] = jnp.zeros_like(modes_odd_ref)
-        for todo in ahead(fields_first_ref, zx_even_ref, back_even_ref, pre_even_ref):
+        for todo in ahead(fields_first_ref, inverse_first_ref, back_even_ref, pre_even_ref):
             todo()
 
-    even = (back_even_ref, pre_even_ref, modes_even_ref)
-    odd = (back_odd_ref, pre_odd_ref, modes_odd_ref)
-    for cell, own, beside in (
-        (
-            0,
-            even,
-            behind(modes_odd_ref, zx_before_ref)
-            + ahead(fields_odd_ref, zx_odd_ref, back_odd_ref, pre_odd_ref),
-        ),
-        (
-            1,
-            odd,
-            behind(modes_even_ref, zx_even_ref)
-            + ahead(fields_next_ref, zx_next_ref, back_even_ref, pre_even_ref),
-        ),
-    ):
-        for o in range(0, channels, 2):
-            if beside:
-                beside.pop(0)()
-            here(cell, *own, o)
-        for todo in beside:
-            todo()
+    even = (0, back_even_ref, pre_even_ref, modes_even_ref)
+    odd = (1, back_odd_ref, pre_odd_ref, modes_odd_ref)
+    beside = {
+        0: ahead(fields_odd_ref, inverse_odd_ref, back_odd_ref, pre_odd_ref)
+        + behind(modes_odd_ref, zx_before_ref),
+        1: ahead(fields_next_ref, inverse_next_ref, back_even_ref, pre_even_ref)
+        + behind(modes_even_ref, zx_even_ref),
+    }
+    items = [(own, o) for own in (even, odd) for o in range(0, channels, 2)]
+    spectral = inverse_pair(back_even_ref, 0)
+    delta = None
+    for n, ((cell, _, pre_ref, modes_ref), o) in enumerate(items):
+        if beside[cell]:
+            beside[cell].pop(0)()
+        if o + 2 >= channels:
+            while beside[cell]:
+                beside[cell].pop(0)()
+        following = None
+        if n + 1 < len(items):
+            (_, back_ref, _, _), later = items[n + 1]
+            following = inverse_pair(back_ref, later)
+        if n > 0:
+            (_, _, _, earlier_ref), earlier = items[n - 1]
+            y_modes(delta, table, earlier_ref, earlier, z_cells)
+        delta = slope_pair(cell, spectral, pre_ref, o)
+        spectral = following
+    y_modes(delta, table, modes_odd_ref, channels - 2, z_cells)
 
     @pl.when(step == last)
     def _():
-        for todo in behind(modes_odd_ref, zx_odd_ref):
+        for todo in behind(modes_odd_ref, zx_last_ref):
             todo()
         store_blocks(total_ref, out_ref, channels)
 
@@ -387,6 +394,7 @@
     rank, table_x, table_zx, table_y = make_tables(x_cells, y_cells, z_cells, slabs)
     lanes = rank * 2 * KZ
     x_upper, x_lower = (jnp.asarray(part) for part in split_parts(table_x))
+    inverse_zx = jnp.asarray(rounded(np.swapaxes(table_zx, 1, 2)))
     table_zx = jnp.asarray(rounded(table_zx))
     y_parts = jnp.asarray(np.concatenate(split_parts(table_y), axis=0))
     inverse_y = jnp.asarray(rounded(table_y.T))
@@ -407,6 +415,9 @@
 
     def zx_at(index, count=1):
         return pl.BlockSpec((count, 2 * z_cells, lanes), lambda x: (index(x), 0, 0))
+
+    def inverse_at(index):
+        return pl.BlockSpec((1, lanes, 2 * z_cells), lambda x: (index(x), 0, 0))
 
     params = pltpu.CompilerParams(
         dimension_semantics=("arbitrary",), vmem_limit_bytes=VMEM_BYTES
@@ -496,8 +507,10 @@
                 whole(inverse_y.shape),
                 zx_at(lambda x: jnp.maximum(2 * x - 1, 0)),
                 zx_at(lambda x: 2 * x),
-                zx_at(lambda x: 2 * x + 1),
-                zx_at(lambda x: jnp.minimum(2 * x + 2, slab_len - 1)),
+                zx_at(lambda x: slab_len - 1),
+                inverse_at(lambda x: 0),
+                inverse_at(lambda x: 2 * x + 1),
+                inverse_at(lambda x: jnp.minimum(2 * x + 2, slab_len - 1)),
             ],
             out_specs=whole(coefs_shape),
             out_shape=coefs_out,
@@ -520,7 +533,9 @@
             table_zx,
             table_zx,
             table_zx,
-            table_zx,
+            inverse_zx,
+            inverse_zx,
+            inverse_zx,
         )
     back = across_samples(back_coefs)
 

time: 258 us -> 225 us (0.87)
  Pallas kernels: 141 us -> 109 us
    pallas_call x1, Pallas kernels: 93.4 us -> 61.1 us  [shards(): pl.pallas_call(slope_kernel, grid=(slab_len // 2,), in_specs=[pl.BlockSpe...]
where the time goes in v3:
time: 225 us
  Pallas kernels  109 us (48%)
  blocking collectives  73.3 us (33%)
  waiting for transfers between devices  27.5 us (12%)
  starting transfers between devices  7.37 us (3%)
  local copies, waits for them, and re-layouts  6.27 us (3%)
    all_to_all x4, blocking collectives, over(): return lax.all_to_all(values, axis, split_axis=0, concat_axis=0, tiled=True)  73.3 us
    pallas_call x1, Pallas kernels, shards(): pl.pallas_call(slope_kernel, grid=(slab_len // 2,), in_specs=[pl.BlockSpe...  61.1 us
    all_to_all x2, waiting for transfers between devices, over(): return lax.all_to_all(values, axis, split_axis=0, concat_axis=0, tiled=True)  27.5 us
    pallas_call x1, Pallas kernels, shards(): pl.pallas_call(forward_kernel, grid=(slab_len // 4,), in_specs=[cells_at(...  18.1 us
    pallas_call x2, Pallas kernels, across_samples(): pl.pallas_call(to_modes_kernel, grid=(data_count // per_step,), in_specs=...  11.9 us
    all_to_all x2, starting transfers between devices, over(): return lax.all_to_all(values, axis, split_axis=0, concat_axis=0, tiled=True)  7.37 us
    pallas_call x1, Pallas kernels, shards(): pl.pallas_call(from_modes_kernel, grid=(slabs,), in_specs=[whole((data_co...  6.97 us
    pallas_call x1, Pallas kernels, shards(): pl.pallas_call(functools.partial(mix_kernel, blocked), out_shape=[jax.Sha...  6.5 us
  transfers between devices with their start and end apart: 2, of which 2 were waited for; matrix products, arithmetic and copies ran while one was open for 2% of the time, Pallas kernels for 0%

profile of v3, /device:TPU:0, one launch (start us, length us, event | category | flops | bytes accessed | tf_op | source)
XLA Modules:
  0.0 224.7 jit_solution(11680029162194011562)
XLA Ops:
  0.0 0.0 copy-start
  0.0 0.8 copy-done
  0.8 18.1 %forward_fields.1 = bf16[4,160,576]{2,1,0:T(8,128)(2,1)S(1)} custom-call(bf16[32,20,128,128]{3,2,1,0:T(8,128)(2,1)} %bitcast.3, bf16[128,128]{1,0:T(8,128)(2,1)S(1)} %copy-done, bf16[32,256,576]{2,1,0:T(8,128)(2,1)} %constant.17.clone.table_zx_ref.zx_before_ref.zx_even_ref.zx_last_ref), custom_call_target="tpu_custom_call" | custom-call | tf_op jit(solution)/shard_map/forward_fields/pallas_call | solution.py:453
  18.9 26.9 %all_to_all.30.coefs_ref = bf16[4,160,576]{2,1,0:T(8,128)(2,1)S(1)} all-to-all(bf16[4,160,576]{2,1,0:T(8,128)(2,1)S(1)} %forward_fields.1), channel_id=1, replica_groups=mesh['dp'=8,'mp'=4] {'mp'}, dimensions={0} | all-to-all | bytes 1474560 | tf_op jit(solution)/shard_map/all_to_all | solution.py:432
  45.8 0.0 copy-start.5
  45.8 0.0 copy-start.3
  45.8 6.4 %shard_map.118 = f32[8,160,128]{2,1,0:T(8,128)} custom-call(bf16[4,160,576]{2,1,0:T(8,128)(2,1)S(1)} %all_to_all.30.coefs_ref, bf16[4,576,1024]{2,1,0:T(8,128)(2,1)} %constant.14.clone.upper_ref, bf16[4,576,1024]{2,1,0:T(8,128)(2,1)} %constant.15.clone.lower_ref), custom_call_target="tpu_custom_call" | custom-call | tf_op jit(solution)/shard_map/pallas_call | solution.py:437
  52.2 3.7 %all-to-all-start.1 = ((f32[8,160,128]{2,1,0:T(8,128)}), f32[8,160,128]{2,1,0:T(8,128)S(1)}, u32[]{:S(2)}, u32[]{:S(2)}) async-start(f32[8,160,128]{2,1,0:T(8,128)} %shard_map.118), calls=%async_computation.1 | async-start | bytes 1310720 | tf_op jit(solution)/shard_map/all_to_all | solution.py:432
  55.9 0.0 copy-done.5
  55.9 0.1 copy.16.weight_ref
  56.0 11.0 %all-to-all-done.1.spectra_ref = f32[8,160,128]{2,1,0:T(8,128)S(1)} async-done(((f32[8,160,128]{2,1,0:T(8,128)}), f32[8,160,128]{2,1,0:T(8,128)S(1)}, u32[]{:S(2)}, u32[]{:S(2)}) %all-to-all-start.1) | async-done | bytes 655392 | tf_op jit(solution)/shard_map/all_to_all | solution.py:432
  67.0 0.0 copy-done.3
  67.0 6.5 %mix_modes.1 = (bf16[8,160,128]{2,1,0:T(8,128)(2,1)S(1)}, f32[8,8,20,128]{3,2,1,0:T(8,128)S(1)}) custom-call(f32[8,160,128]{2,1,0:T(8,128)S(1)} %all-to-all-done.1.spectra_ref, bf16[4,2,20,20,128]{4,3,2,1,0:T(8,128)(2,1)S(1)} %copy.16.weight_ref, f32[1,128]{1,0:T(1,128)S(1)} %copy-done.3), custom_call_target="tpu_custom_call" | custom-call | tf_op jit(solution)/shard_map/mix_modes/pallas_call | solution.py:471
  73.6 10.0 %all_to_all.31.modes_ref = bf16[8,160,128]{2,1,0:T(8,128)(2,1)S(1)} all-to-all(bf16[8,160,128]{2,1,0:T(8,128)(2,1)S(1)} %get-tuple-element.8), channel_id=1, replica_groups=mesh['dp'=8,'mp'=4] {'dp'}, dimensions={0} | all-to-all | bytes 655360 | tf_op jit(solution)/shard_map/all_to_all | solution.py:432
  83.6 0.0 copy-start.6
  83.6 7.0 %shard_map.119 = bf16[4,160,576]{2,1,0:T(8,128)(2,1)} custom-call(bf16[8,160,128]{2,1,0:T(8,128)(2,1)S(1)} %all_to_all.31.modes_ref, bf16[4,576,1024]{2,1,0:T(8,128)(2,1)} %constant.14.clone.upper_ref, bf16[4,576,1024]{2,1,0:T(8,128)(2,1)} %constant.15.clone.lower_ref), custom_call_target="tpu_custom_call" | custom-call | tf_op jit(solution)/shard_map/pallas_call | solution.py:484
  90.5 0.0 copy-start.1
  90.6 3.6 %all-to-all-start.3 = ((bf16[4,160,576]{2,1,0:T(8,128)(2,1)}), bf16[4,160,576]{2,1,0:T(8,128)(2,1)S(1)}, u32[]{:S(2)}, u32[]{:S(2)}) async-start(bf16[4,160,576]{2,1,0:T(8,128)(2,1)} %shard_map.119), calls=%async_computation.3 | async-start | bytes 1638400 | tf_op jit(solution)/shard_map/all_to_all | solution.py:432
  94.2 0.0 copy-done.6
  94.2 0.1 copy.17
  94.3 1.5 broadcast_multiply_fusion
  95.8 2.8 %mul.27.conv_ref = bf16[320,320]{1,0:T(8,128)(2,1)S(1)} reshape(bf16[20,16,20,16]{3,2,1,0:T(8,128)(2,1)} %broadcast_multiply_fusion) | data formatting | bytes 409600 | tf_op jit(solution)/shard_map/jit(kron)/mul | solution.py:403
  98.7 16.5 %all-to-all-done.3.mixed_ref = bf16[4,160,576]{2,1,0:T(8,128)(2,1)S(1)} async-done(((bf16[4,160,576]{2,1,0:T(8,128)(2,1)}), bf16[4,160,576]{2,1,0:T(8,128)(2,1)S(1)}, u32[]{:S(2)}, u32[]{:S(2)}) %all-to-all-start.3) | async-done | bytes 737312 | tf_op jit(solution)/shard_map/all_to_all | solution.py:432
  115.2 0.0 copy-done.1
  115.2 0.0 copy-done.2
  115.2 0.0 copy-done.4
  115.2 61.1 %slope_and_back.1 = bf16[4,160,576]{2,1,0:T(8,128)(2,1)S(1)} custom-call(f32[20]{0:T(128)S(1)} %copy-done.4, bf16[32,20,128,128]{3,2,1,0:T(8,128)(2,1)} %bitcast.4, bf16[32,20,128,128]{3,2,1,0:T(8,128)(2,1)} %bitcast.5, bf16[32,20,128,128]{3,2,1,0:T(8,128)(2,1)} %bitcast.6, bf16[32,20,128,128]{3,2,1,0:T(8,128)(2,1)} %bitcast.7, ...), custom_call_target="tpu_custom_call" | custom-call | tf_op jit(solution)/shard_map/slope_and_back/pallas_call | solution.py:495
  176.3 22.8 %all_to_all.32.coefs_ref = bf16[4,160,576]{2,1,0:T(8,128)(2,1)S(1)} all-to-all(bf16[4,160,576]{2,1,0:T(8,128)(2,1)S(1)} %slope_and_back.1), channel_id=1, replica_groups=mesh['dp'=8,'mp'=4] {'mp'}, dimensions={0} | all-to-all | bytes 1474560 | tf_op jit(solution)/shard_map/all_to_all | solution.py:432
  199.1 5.6 %shard_map.120 = f32[8,160,128]{2,1,0:T(8,128)S(1)} custom-call(bf16[4,160,576]{2,1,0:T(8,128)(2,1)S(1)} %all_to_all.32.coefs_ref, bf16[4,576,1024]{2,1,0:T(8,128)(2,1)} %constant.14.clone.upper_ref, bf16[4,576,1024]{2,1,0:T(8,128)(2,1)} %constant.15.clone.lower_ref), custom_call_target="tpu_custom_call" | custom-call | tf_op jit(solution)/shard_map/pallas_call | solution.py:437
  204.6 13.5 %all_to_all.33.back_ref = f32[8,160,128]{2,1,0:T(8,128)S(1)} all-to-all(f32[8,160,128]{2,1,0:T(8,128)S(1)} %shard_map.120), channel_id=1, replica_groups=mesh['dp'=8,'mp'=4] {'dp'}, dimensions={0} | all-to-all | bytes 1310720 | tf_op jit(solution)/shard_map/all_to_all | solution.py:432
  218.2 4.0 %weight_gradient.1 = f32[4,2,20,20,128]{4,3,2,1,0:T(8,128)S(1)} custom-call(f32[8,8,20,128]{3,2,1,0:T(8,128)S(1)} %get-tuple-element.7.spectra_ref, f32[8,160,128]{2,1,0:T(8,128)S(1)} %all_to_all.33.back_ref, f32[1,128]{1,0:T(1,128)S(1)} %copy-done.3), custom_call_target="tpu_custom_call" | custom-call | tf_op jit(solution)/shard_map/weight_gradient/pallas_call | solution.py:543
  222.2 2.4 %copy.18 = f32[4,2,20,20,128]{4,1,3,2,0:T(2,128)} copy(f32[4,2,20,20,128]{4,3,2,1,0:T(8,128)S(1)} %weight_gradient.1) | data formatting | bytes 3276800 | tf_op jit(solution)/shard_map/weight_gradient/pallas_call | solution.py:543
  (3 shorter events, 0.0 us)
Async XLA Ops:
  0.0 0.8 copy-start
  45.8 10.1 %copy-start.5 = (bf16[4,2,20,20,128]{4,1,3,2,0:T(2,128)(2,1)S(1)}, bf16[4,2,20,20,128]{4,1,3,2,0:T(2,128)(2,1)}, u32[]{:S(2)}) copy-start(bf16[4,2,20,20,128]{4,1,3,2,0:T(2,128)(2,1)} %param.14) | copy-start | bytes 2457604
  45.8 21.3 %copy-start.3 = (f32[1,128]{1,0:T(1,128)S(1)}, f32[1,128]{1,0:T(1,128)}, u32[]{:S(2)}) copy-start(f32[1,128]{1,0:T(1,128)} %constant.20.clone.scale_ref) | copy-start | bytes 1540
  52.2 14.9 %all-to-all-start.1 = ((f32[8,160,128]{2,1,0:T(8,128)}), f32[8,160,128]{2,1,0:T(8,128)S(1)}, u32[]{:S(2)}, u32[]{:S(2)}) async-start(f32[8,160,128]{2,1,0:T(8,128)} %shard_map.118), calls=%async_computation.1 | async-start | bytes 1310720 | tf_op jit(solution)/shard_map/all_to_all | solution.py:432
  83.6 10.6 %copy-start.6 = (bf16[20,20]{1,0:T(8,128)(2,1)S(1)}, bf16[20,20]{1,0:T(8,128)(2,1)}, u32[]{:S(2)}) copy-start(bf16[20,20]{1,0:T(8,128)(2,1)} %param.15) | copy-start | bytes 2404
  90.5 24.6 %copy-start.1 = (bf16[128,128]{1,0:T(8,128)(2,1)S(1)}, bf16[128,128]{1,0:T(8,128)(2,1)}, u32[]{:S(2)}) copy-start(bf16[128,128]{1,0:T(8,128)(2,1)} %constant.18.clone.table_y_ref) | copy-start | bytes 98308
  90.5 24.6 %copy-start.2 = (bf16[128,64]{1,0:T(8,128)(2,1)S(1)}, bf16[128,64]{1,0:T(8,128)(2,1)}, u32[]{:S(2)}) copy-start(bf16[128,64]{1,0:T(8,128)(2,1)} %constant.19.clone.inverse_y_ref) | copy-start | bytes 49156
  90.5 24.6 %copy-start.4 = (f32[20]{0:T(128)S(1)}, f32[20]{0:T(128)}, u32[]{:S(2)}) copy-start(f32[20]{0:T(128)} %bias_ref.1) | copy-start | bytes 244
  90.6 24.6 %all-to-all-start.3 = ((bf16[4,160,576]{2,1,0:T(8,128)(2,1)}), bf16[4,160,576]{2,1,0:T(8,128)(2,1)S(1)}, u32[]{:S(2)}, u32[]{:S(2)}) async-start(bf16[4,160,576]{2,1,0:T(8,128)(2,1)} %shard_map.119), calls=%async_computation.3 | async-start | bytes 1638400 | tf_op jit(solution)/shard_map/all_to_all | solution.py:432
